TPU v7x, 32 devices: a whole 2x2x4 slice. The times are simulated.
32 devices in a mesh: sy: 4 (over z), sx: 4 (over y, core), tp: 2 (over x).
Axes of the slice: x: 2, y: 2, z: 4, core: 2. Of those that a mesh axis runs over, the one named last changes fastest.
Arguments:
- features: bfloat16 [96, 64, 1408], P('sy', 'sx', 'tp'), may hold values from -6 to 6
- depth_kernel: float32 [7, 7, 1408], P(None, None, 'tp'), may hold values from -0.875 to 0.875
- depth_bias: float32 [1408], P('tp'), may hold values from -1 to 1
- norm_gain: float32 [1408], replicated, may hold values from 0.1 to 1.9
- norm_bias: float32 [1408], replicated, may hold values from -3 to 3
- up_weight: bfloat16 [1408, 5632], P(None, 'tp'), may hold values from -0.15625 to 0.15625
- up_bias: float32 [5632], P('tp'), may hold values from -3 to 3
- response_gain: float32 [5632], P('tp'), may hold values from -4 to 4
- response_shift: float32 [5632], P('tp'), may hold values from -3 to 3
- down_weight: bfloat16 [5632, 1408], P('tp', ('sy', 'sx')), may hold values from -0.078125 to 0.078125
- down_bias: float32 [1408], P('tp'), may hold values from -3 to 3
- tissue: int32 [12, 8], P('sy', 'sx'), may hold values from 0 to 1, as said below
- cotangent: bfloat16 [96, 64, 1408], P('sy', 'sx', 'tp'), may hold values from -6 to 6
Outputs:
- block_out: bfloat16 [96, 64, 1408], P('sy', 'sx', 'tp')
- feature_grad: bfloat16 [96, 64, 1408], P('sy', 'sx', 'tp')
Inputs may be any that keep to these rules, and one draw needn't show every extreme that they name: Each device's block of 3 x 2 tiles holds 1 to 4 tissue tiles; some device's block holds exactly 4.
All inputs are finite; a program needn't handle non-finite values.
Results may differ from a plain program's by a relative error of at most 0.0049.
The roundings to bfloat16 on the way count: a program that leaves them out, or rounds other values in their place, can miss the bound.
Values may be sent and summed in bfloat16 or wider, within the bound.
A program may use at most 128 MiB of HBM per device.

v0:
```python
import jax
import jax.numpy as jnp
from jax import lax
from jax.sharding import PartitionSpec as P

KERNEL = 7
TILE = 8


root_half = 0.7071067811865476
root_two_pi_inv = 0.3989422804014327


def extended(block, sides, width):
    for axis, dim in sides:
        count = lax.axis_size(axis)
        forward = [(i, i + 1) for i in range(count - 1)]
        backward = [(target, source) for source, target in forward]
        low = lax.ppermute(
            lax.slice_in_dim(block, block.shape[dim] - width, None, axis=dim), axis, forward
        )
        high = lax.ppermute(lax.slice_in_dim(block, 0, width, axis=dim), axis, backward)
        block = jnp.concatenate([low, block, high], axis=dim)
    return block


def gelu_value(values):
    return 0.5 * values * (1.0 + jax.scipy.special.erf(values * root_half))


def gelu_slope(values):
    return (
        0.5 * (1.0 + jax.scipy.special.erf(values * root_half))
        + values * jnp.exp(-0.5 * values * values) * root_two_pi_inv
    )


def depthwise(padded, kernel, rows_out, cols_out, flipped):
    summed = jnp.zeros((rows_out, cols_out, kernel.shape[2]), jnp.float32)
    last_tap = KERNEL - 1
    for row_tap in range(KERNEL):
        for col_tap in range(KERNEL):
            row_start = last_tap - row_tap if flipped else row_tap
            col_start = last_tap - col_tap if flipped else col_tap
            window = padded[row_start : row_start + rows_out, col_start : col_start + cols_out]
            summed = summed + window.astype(jnp.float32) * kernel[row_tap, col_tap]
    return summed


def extend(image):
    return extended(image, (("sy", 0), ("sx", 1)), KERNEL // 2)


def all_channels(rows_array):
    return lax.all_gather(rows_array, "tp", axis=1, tiled=True)


def global_vector(local_part):
    hidden_local = local_part.shape[0]
    placed = lax.dynamic_update_slice(
        jnp.zeros((hidden_local * lax.axis_size("tp"),), jnp.float32),
        local_part,
        (lax.axis_index("tp") * hidden_local,),
    )
    return lax.psum(placed, ("sy", "sx", "tp"))


def shards(
    features,
    depth_kernel,
    depth_bias,
    norm_gain,
    norm_bias,
    up_weight,
    up_bias,
    response_gain,
    response_shift,
    down_weight,
    down_bias,
    tissue,
    cotangent,
):
    image_rows, image_cols, local_channels = features.shape
    hidden_local = up_weight.shape[1]
    channel_start = lax.axis_index("tp") * local_channels
    contract_last = (((1,), (1,)), ((), ()))
    pixel_mask = jnp.repeat(jnp.repeat(tissue, TILE, axis=0), TILE, axis=1).astype(jnp.float32)
    mask_rows = pixel_mask.reshape(-1)

    def select(image):
        return image.reshape(image_rows * image_cols, image.shape[2])

    def restore(rows_array):
        return rows_array.reshape(image_rows, image_cols, rows_array.shape[1])

    convolved = (
        depthwise(extend(features), depth_kernel, image_rows, image_cols, False) + depth_bias
    ).astype(jnp.bfloat16)
    gathered = all_channels(select(convolved)).astype(jnp.float32)
    centre = jnp.mean(gathered, axis=1, keepdims=True)
    spread = jnp.mean(jnp.square(gathered - centre), axis=1, keepdims=True)
    inv_scale = lax.rsqrt(spread + 1e-06)
    standard = (gathered - centre) * inv_scale
    normed = (standard * norm_gain + norm_bias).astype(jnp.bfloat16)
    preact = jnp.dot(normed, up_weight, preferred_element_type=jnp.float32) + up_bias
    hidden = gelu_value(preact).astype(jnp.bfloat16)
    hidden_wide = hidden.astype(jnp.float32)
    squares = global_vector(jnp.sum(mask_rows[:, None] * hidden_wide * hidden_wide, axis=0))
    all_norms = jnp.sqrt(squares)
    norm_level = jnp.mean(all_norms) + 1e-06
    unit_start = lax.axis_index("tp") * hidden_local
    column_norms = lax.dynamic_slice_in_dim(all_norms, unit_start, hidden_local)
    norm_ratio = column_norms / norm_level
    response = (response_gain * hidden_wide * norm_ratio + response_shift + hidden_wide).astype(
        jnp.bfloat16
    )
    down_whole = lax.all_gather(down_weight, ("sy", "sx"), axis=1, tiled=True)
    partial_out = jnp.dot(response, down_whole, preferred_element_type=jnp.float32)
    branch = lax.psum_scatter(partial_out, "tp", scatter_dimension=1, tiled=True)
    branch_image = restore(branch + down_bias)
    block_out = (features.astype(jnp.float32) + pixel_mask[:, :, None] * branch_image).astype(
        jnp.bfloat16
    )
    masked_cot = (select(cotangent).astype(jnp.float32) * mask_rows[:, None]).astype(jnp.bfloat16)
    cot_wide = all_channels(masked_cot)
    back_hidden = lax.dot_general(
        cot_wide, down_whole, contract_last, preferred_element_type=jnp.float32
    )
    ratio_grad = global_vector(response_gain * jnp.sum(back_hidden * hidden_wide, axis=0))
    ratio_local = lax.dynamic_slice_in_dim(ratio_grad, unit_start, hidden_local)
    norms_grad = ratio_local / norm_level - jnp.sum(ratio_grad * all_norms) / (
        all_norms.shape[0] * norm_level * norm_level
    )
    hidden_grad = (
        back_hidden * (response_gain * norm_ratio + 1.0)
        + norms_grad * mask_rows[:, None] * hidden_wide / column_norms
    )
    preact_grad = (hidden_grad * gelu_slope(preact)).astype(jnp.bfloat16)
    grad_terms = lax.dot_general(
        preact_grad, up_weight, contract_last, preferred_element_type=jnp.float32
    )
    normed_grad = lax.psum(grad_terms, "tp")
    scaled = normed_grad * norm_gain
    convolved_grad = inv_scale * (
        scaled
        - jnp.mean(scaled, axis=1, keepdims=True)
        - standard * jnp.mean(scaled * standard, axis=1, keepdims=True)
    )
    convolved_grad = convolved_grad.astype(jnp.bfloat16)
    local_grad = lax.dynamic_slice_in_dim(convolved_grad, channel_start, local_channels, 1)
    grad_image = restore(local_grad)
    feature_grad = (
        cotangent.astype(jnp.float32)
        + depthwise(extend(grad_image), depth_kernel, image_rows, image_cols, True)
    ).astype(jnp.bfloat16)
    return (block_out, feature_grad)


def solution(mesh):
    placed = (
        P("sy", "sx", "tp"),
        P(None, None, "tp"),
        P("tp"),
        P(),
        P(),
        P(None, "tp"),
        P("tp"),
        P("tp"),
        P("tp"),
        P("tp", ("sy", "sx")),
        P("tp"),
        P("sy", "sx"),
        P("sy", "sx", "tp"),
    )
    return jax.shard_map(
        shards,
        mesh=mesh,
        in_specs=placed,
        out_specs=(P("sy", "sx", "tp"), P("sy", "sx", "tp")),
        check_vma=False,
    )
```

profile of v0, /device:TPU:12, one launch (start us, length us, event | category | flops | bytes accessed | tf_op | source)
XLA Modules:
  0.0 336.7 jit_solution(16324802515780690744)
XLA Ops:
  8.1 3.5 %collective-permute-start = (bf16[3,16,704]{2,1,0:T(8,128)(2,1)S(1)}, bf16[3,16,704]{2,1,0:T(8,128)(2,1)S(1)}, u32[]{:S(2)}, u32[]{:S(2)}) collective-permute-start(bf16[3,16,704]{2,1,0:T(8,128)(2,1)S(1)} %get-tuple-element.77), channel_id=1, source_target_pairs={{0,8},{8,16},{16,24},{1,9},{9,17},{17,25},{2,10},{10,18},{18,26},{... | collective-permute-start | bytes 202760 | tf_op jit(solution)/shard_map/ppermute | solution.py:19
  11.6 2.4 collective-permute-start.1
  14.0 1.4 slice_reduce_fusion.48
  15.4 1.1 slice_reduce_fusion.46
  16.6 1.2 constant_dynamic-update-slice_fusion.3
  18.1 1.9 collective-permute-start.2
  20.0 3.6 %collective-permute-start.3 = (bf16[30,3,704]{2,1,0:T(4,128)(2,1)S(1)}, bf16[30,3,704]{2,1,0:T(4,128)(2,1)S(1)}, u32[]{:S(2)}, u32[]{:S(2)}) collective-permute-start(bf16[30,3,704]{2,1,0:T(4,128)(2,1)S(1)} %get-tuple-element.70), channel_id=1, source_target_pairs={{2,0},{4,2},{6,4},{3,1},{5,3},{7,5},{10,8},{12,10},{14,12},{11,9},... | collective-permute-start | bytes 380168 | tf_op jit(solution)/shard_map/ppermute | solution.py:22
  23.6 1.4 slice_reduce_fusion.47
  25.0 1.6 collective-permute-done.3
  26.7 14.1 %add_convert_fusion.2 = bf16[24,16,704]{2,1,0:T(8,128)(2,1)S(1)} fusion(bf16[24,16,704]{2,1,0:T(8,128)(2,1)S(1)} %copy-done, bf16[30,16,704]{2,1,0:T(8,128)(2,1)S(1)} %get-tuple-element.81, bf16[30,3,704]{2,1,0:T(4,128)(2,1)S(1)} %collective-permute-done.3, bf16[30,3,704]{2,1,0:T(4,128)(2,1)S(1)} %collective-permute-done.2, ...), kind=kLoop, calls=%fused_computation.149 | loop fusion | flops 74072064 | bytes 5395456 | tf_op jit(solution)/shard_map/convert_element_type | solution.py:98
  40.8 1.0 copy.21
  44.3 20.9 %all-gather.4.cloned.1.call-done = bf16[384,1408]{0,1:T(8,128)(2,1)} async-done(((bf16[384,704]{0,1:T(8,128)(2,1)}), bf16[384,1408]{0,1:T(8,128)(2,1)}) %all-gather.4.cloned.1.call-update) | async-done | bytes 1081360 | tf_op jit(solution)/shard_map/all_gather | solution.py:55
  65.2 1.7 copy.22
  67.6 8.6 %convolution_add_fusion = f32[384,2816]{1,0:T(8,128)} fusion(bf16[1408,2816]{1,0:T(8,128)(2,1)} %param.18, f32[2816]{0:T(1024)S(1)} %copy-done.7, f32[1408]{0:T(1024)S(1)} %copy-done.9, f32[1408]{0:T(1024)S(1)} %copy-done.3, bf16[384,1408]{1,0:T(8,128)(2,1)S(1)} %copy.22, f32[384]{0:T(512)S(1)} %add_rsqrt_fusion, f32[384]{0:T(512)S(1)} %broadcast_multiply_fusion.3), kind=kOutput, calls=%fused_computation.62 | convolution fusion | flops 3049390080 | bytes 13362176 | tf_op jit(solution)/shard_map/dot_general | solution.py:105
  76.2 12.8 %all-gather.8.cloned.1.call-done = bf16[384,1408]{0,1:T(8,128)(2,1)} async-done(((bf16[384,704]{0,1:T(8,128)(2,1)}), bf16[384,1408]{0,1:T(8,128)(2,1)}) %all-gather.8.cloned.1.call-update) | async-done | bytes 1081360 | tf_op jit(solution)/shard_map/all_gather | solution.py:55
  89.0 72.9 %all-gather.6.cloned.1.call-done = bf16[2816,1408]{0,1:T(8,128)(2,1)} async-done(((bf16[2816,88]{0,1:T(8,128)(2,1)}), bf16[2816,1408]{0,1:T(8,128)(2,1)}) %all-gather.6.cloned.1.call-update) | async-done | bytes 7929872 | tf_op jit(solution)/shard_map/all_gather | solution.py:117
  161.9 9.9 %fusion.10 = (f32[2816]{0:T(1024)S(1)}, f32[2816]{0:T(1024)S(1)}, bf16[384,2816]{1,0:T(8,128)(2,1)}, f32[384,2816]{1,0:T(8,128)}) fusion(f32[384]{0:T(512)S(1)} %convert_element_type.419, f32[384,2816]{1,0:T(8,128)} %convolution_add_fusion, bf16[384,1408]{0,1:T(8,128)(2,1)} %all-gather.8.cloned.1.call-done, bf16[2816,1408]{0,1:T(8,128)(2,1)} %all-gather.6.cloned.1.call-done), kind=kOutput, calls=%fused_computation.57 | convolution fusion | flops 3056953856 | bytes 19848704 | tf_op jit(solution)/shard_map/dot_general | solution.py:126
  172.2 41.2 %all-reduce = (f32[5632]{0:T(1024)S(1)}, f32[5632]{0:T(1024)S(1)}) all-reduce(f32[5632]{0:T(1024)S(1)} %dynamic_update_slice.6, f32[5632]{0:T(1024)S(1)} %multiply_dynamic-update-slice_fusion), channel_id=1, replica_groups=mesh['sy'=4,'sx'=4,'tp'=2] {'sy','sx','tp'}, use_global_device_ids=true, to_apply=%region_3.0 | all-reduce | flops 11264 | bytes 90112 | tf_op jit(solution)/shard_map/psum | solution.py:65
  215.4 12.4 %fusion.21 = f32[384,1408]{1,0:T(8,128)} fusion(bf16[1408,2816]{1,0:T(8,128)(2,1)} %param.18, f32[384,2816]{1,0:T(8,128)} %convolution_add_fusion, bf16[384,2816]{1,0:T(8,128)(2,1)} %get-tuple-element.63, f32[384,2816]{1,0:T(8,128)} %get-tuple-element.83, f32[2816]{0:T(1024)S(1)} %get-tuple-element.62, f32[2816]{0:T(1024)S(1)} %get-tuple-element.84, ...), kind=kOutput, calls=%fused_computation.74 | convolution fusion | flops 3062366208 | bytes 20941312 | tf_op jit(solution)/shard_map/dot_general | solution.py:139
  228.5 9.6 %fusion.16 = f32[384,1408]{0,1:T(8,128)} fusion(bf16[2816,1408]{0,1:T(8,128)(2,1)} %all-gather.6.cloned.1.call-done, bf16[384,2816]{1,0:T(8,128)(2,1)} %get-tuple-element.63, f32[2816]{0:T(1024)S(1)} %copy-done.8, f32[2816]{0:T(1024)S(1)} %get-tuple-element.61, f32[2816]{0:T(1024)S(1)} %copy-done.2), kind=kOutput, calls=%fused_computation.68 | convolution fusion | flops 3051552768 | bytes 12289024 | tf_op jit(solution)/shard_map/dot_general | solution.py:118
  238.1 54.4 %all-reduce.3.cloned.1.call-done = f32[384,1408]{1,0:T(8,128)} async-done(((f32[384,1408]{1,0:T(8,128)}), f32[384,1408]{1,0:T(8,128)}) %all-reduce.3.cloned.1.call-update) | async-done | bytes 2162704 | tf_op jit(solution)/shard_map/psum | solution.py:142
  292.5 2.3 fusion.102
  295.8 3.4 %collective-permute-start.4 = (bf16[3,16,704]{2,1,0:T(8,128)(2,1)S(1)}, bf16[3,16,704]{2,1,0:T(8,128)(2,1)S(1)}, u32[]{:S(2)}, u32[]{:S(2)}) collective-permute-start(bf16[3,16,704]{2,1,0:T(8,128)(2,1)S(1)} %bitcast.23), channel_id=1, source_target_pairs={{0,8},{8,16},{16,24},{1,9},{9,17},{17,25},{2,10},{10,18},{18,26},{... | collective-permute-start | bytes 202760 | tf_op jit(solution)/shard_map/ppermute | solution.py:19
  299.2 2.4 collective-permute-start.5
  302.0 3.4 %collective-permute-done.5 = bf16[3,16,704]{2,1,0:T(8,128)(2,1)S(1)} collective-permute-done((bf16[3,16,704]{2,1,0:T(8,128)(2,1)S(1)}, bf16[3,16,704]{2,1,0:T(8,128)(2,1)S(1)}, u32[]{:S(2)}, u32[]{:S(2)}) %collective-permute-start.5) | collective-permute-done | bytes 67616 | tf_op jit(solution)/shard_map/ppermute | solution.py:22
  305.6 1.9 collective-permute-start.6
  307.5 2.6 collective-permute-start.7
  310.6 3.8 %collective-permute-done.7 = bf16[30,3,704]{2,1,0:T(4,128)(2,1)S(1)} collective-permute-done((bf16[30,3,704]{2,1,0:T(4,128)(2,1)S(1)}, bf16[30,3,704]{2,1,0:T(4,128)(2,1)S(1)}, u32[]{:S(2)}, u32[]{:S(2)}) %collective-permute-start.7) | collective-permute-done | bytes 126752 | tf_op jit(solution)/shard_map/ppermute | solution.py:19
  315.0 10.3 %add_convert_fusion.1 = bf16[24,16,704]{2,1,0:T(8,128)(2,1)} fusion(bf16[24,16,704]{2,1,0:T(8,128)(2,1)S(1)} %bitcast.18, bf16[3,16,704]{2,1,0:T(8,128)(2,1)S(1)} %collective-permute-done.4, bf16[3,16,704]{2,1,0:T(8,128)(2,1)S(1)} %collective-permute-done.5, bf16[30,19,704]{2,1,0:T(8,128)(2,1)S(1)} %get-tuple-element.66, ...), kind=kLoop, calls=%fused_computation.148 | loop fusion | flops 41902080 | bytes 24603392 | tf_op jit(solution)/shard_map/convert_element_type | solution.py:155
  325.3 2.0 reduce-scatter.2.cloned.1.call-done
  327.3 1.4 broadcast_add_fusion
  329.1 1.0 fusion.48
  (66 shorter events, 9.1 us)
Async XLA Ops:
  7.2 58.0 %all-gather.4.cloned.1.call-start = ((), (), s32[]{:S(2)}) async-start(), calls=%async_computation.1 | async-start | bytes 1622016 | tf_op jit(solution)/shard_map/all_gather | solution.py:55
  8.1 8.4 %collective-permute-start = (bf16[3,16,704]{2,1,0:T(8,128)(2,1)S(1)}, bf16[3,16,704]{2,1,0:T(8,128)(2,1)S(1)}, u32[]{:S(2)}, u32[]{:S(2)}) collective-permute-start(bf16[3,16,704]{2,1,0:T(8,128)(2,1)S(1)} %get-tuple-element.77), channel_id=1, source_target_pairs={{0,8},{8,16},{16,24},{1,9},{9,17},{17,25},{2,10},{10,18},{18,26},{... | collective-permute-start | bytes 202760 | tf_op jit(solution)/shard_map/ppermute | solution.py:19
  11.6 6.2 %collective-permute-start.1 = (bf16[3,16,704]{2,1,0:T(8,128)(2,1)S(1)}, bf16[3,16,704]{2,1,0:T(8,128)(2,1)S(1)}, u32[]{:S(2)}, u32[]{:S(2)}) collective-permute-start(bf16[3,16,704]{2,1,0:T(8,128)(2,1)S(1)} %get-tuple-element.76), channel_id=1, source_target_pairs={{8,0},{16,8},{24,16},{9,1},{17,9},{25,17},{10,2},{18,10},{26,18},{... | collective-permute-start | bytes 202760 | tf_op jit(solution)/shard_map/ppermute | solution.py:22
  17.8 8.9 %copy-start = (bf16[24,16,704]{2,1,0:T(8,128)(2,1)S(1)}, bf16[24,16,704]{2,1,0:T(8,128)(2,1)}, u32[]{:S(2)}) copy-start(bf16[24,16,704]{2,1,0:T(8,128)(2,1)} %param.13) | copy-start | bytes 1622020
  17.8 8.9 %copy-start.5 = (f32[704]{0:T(1024)S(1)}, f32[704]{0:T(1024)}, u32[]{:S(2)}) copy-start(f32[704]{0:T(1024)} %param.15) | copy-start | bytes 8452
  18.1 7.0 %collective-permute-start.2 = (bf16[30,3,704]{2,1,0:T(4,128)(2,1)S(1)}, bf16[30,3,704]{2,1,0:T(4,128)(2,1)S(1)}, u32[]{:S(2)}, u32[]{:S(2)}) collective-permute-start(bf16[30,3,704]{2,1,0:T(4,128)(2,1)S(1)} %get-tuple-element.69), channel_id=1, source_target_pairs={{0,2},{2,4},{4,6},{1,3},{3,5},{5,7},{8,10},{10,12},{12,14},{9,11},... | collective-permute-start | bytes 380168 | tf_op jit(solution)/shard_map/ppermute | solution.py:19
  20.0 6.7 %collective-permute-start.3 = (bf16[30,3,704]{2,1,0:T(4,128)(2,1)S(1)}, bf16[30,3,704]{2,1,0:T(4,128)(2,1)S(1)}, u32[]{:S(2)}, u32[]{:S(2)}) collective-permute-start(bf16[30,3,704]{2,1,0:T(4,128)(2,1)S(1)} %get-tuple-element.70), channel_id=1, source_target_pairs={{2,0},{4,2},{6,4},{3,1},{5,3},{7,5},{10,8},{12,10},{14,12},{11,9},... | collective-permute-start | bytes 380168 | tf_op jit(solution)/shard_map/ppermute | solution.py:22
  40.8 1.1 copy-start.6
  40.8 1.6 copy-start.1
  41.8 47.2 %all-gather.8.cloned.1.call-start = ((), (), s32[]{:S(2)}) async-start(), calls=%async_computation.4 | async-start | bytes 1622016 | tf_op jit(solution)/shard_map/all_gather | solution.py:55
  43.5 118.4 %all-gather.6.cloned.1.call-start = ((), (), s32[]{:S(2)}) async-start(), calls=%async_computation.2 | async-start | bytes 8425472 | tf_op jit(solution)/shard_map/all_gather | solution.py:117
  44.2 248.3 %all-reduce.3.cloned.1.call-start = ((), (), s32[]{:S(2)}) async-start(), calls=%async_computation.5 | async-start | bytes 4325376 | tf_op jit(solution)/shard_map/psum | solution.py:142
  66.9 0.7 copy-start.3
  66.9 0.7 copy-start.7
  66.9 0.7 copy-start.9
  76.2 95.8 %copy-start.2 = (f32[2816]{0:T(1024)S(1)}, f32[2816]{0:T(1024)}, u32[]{:S(2)}) copy-start(f32[2816]{0:T(1024)} %param.20) | copy-start | bytes 33796
  227.8 0.7 copy-start.8
  227.8 99.5 %reduce-scatter.2.cloned.1.call-start = ((), (), s32[]{:S(2)}) async-start(), calls=%async_computation.3 | async-start | bytes 3244032 | tf_op jit(solution)/shard_map/reduce_scatter | solution.py:119
  295.8 6.2 %collective-permute-start.4 = (bf16[3,16,704]{2,1,0:T(8,128)(2,1)S(1)}, bf16[3,16,704]{2,1,0:T(8,128)(2,1)S(1)}, u32[]{:S(2)}, u32[]{:S(2)}) collective-permute-start(bf16[3,16,704]{2,1,0:T(8,128)(2,1)S(1)} %bitcast.23), channel_id=1, source_target_pairs={{0,8},{8,16},{16,24},{1,9},{9,17},{17,25},{2,10},{10,18},{18,26},{... | collective-permute-start | bytes 202760 | tf_op jit(solution)/shard_map/ppermute | solution.py:19
  299.2 6.2 %collective-permute-start.5 = (bf16[3,16,704]{2,1,0:T(8,128)(2,1)S(1)}, bf16[3,16,704]{2,1,0:T(8,128)(2,1)S(1)}, u32[]{:S(2)}, u32[]{:S(2)}) collective-permute-start(bf16[3,16,704]{2,1,0:T(8,128)(2,1)S(1)} %bitcast.22), channel_id=1, source_target_pairs={{8,0},{16,8},{24,16},{9,1},{17,9},{25,17},{10,2},{18,10},{26,18},{... | collective-permute-start | bytes 202760 | tf_op jit(solution)/shard_map/ppermute | solution.py:22
  305.6 5.0 %collective-permute-start.6 = (bf16[30,3,704]{2,1,0:T(4,128)(2,1)S(1)}, bf16[30,3,704]{2,1,0:T(4,128)(2,1)S(1)}, u32[]{:S(2)}, u32[]{:S(2)}) collective-permute-start(bf16[30,3,704]{2,1,0:T(4,128)(2,1)S(1)} %get-tuple-element.67), channel_id=1, source_target_pairs={{2,0},{4,2},{6,4},{3,1},{5,3},{7,5},{10,8},{12,10},{14,12},{11,9},... | collective-permute-start | bytes 380168 | tf_op jit(solution)/shard_map/ppermute | solution.py:22
  307.5 6.9 %collective-permute-start.7 = (bf16[30,3,704]{2,1,0:T(4,128)(2,1)S(1)}, bf16[30,3,704]{2,1,0:T(4,128)(2,1)S(1)}, u32[]{:S(2)}, u32[]{:S(2)}) collective-permute-start(bf16[30,3,704]{2,1,0:T(4,128)(2,1)S(1)} %get-tuple-element.68), channel_id=1, source_target_pairs={{0,2},{2,4},{4,6},{1,3},{3,5},{5,7},{8,10},{10,12},{12,14},{9,11},... | collective-permute-start | bytes 380168 | tf_op jit(solution)/shard_map/ppermute | solution.py:19
  314.9 12.4 %copy-start.4 = (f32[704]{0:T(1024)S(1)}, f32[704]{0:T(1024)}, u32[]{:S(2)}) copy-start(f32[704]{0:T(1024)} %param.23) | copy-start | bytes 8452
Sparse Core Ops, SparseCore 0:
  42.0 23.1 all-gather.3
  67.3 21.6 all-gather.7
  91.2 70.6 all-gather.5
  227.9 64.5 all-reduce.2
  294.7 32.5 reduce-scatter.1
where the time goes:
time: 339 us; the launch traced here: 337 us
  waiting for transfers between devices  173 us (51%)
  blocking collectives  41.2 us (12%)
  matrix products  40.4 us (12%)
  other arithmetic  33.2 us (10%)
  starting transfers between devices  22 us (6%)
  between operations  15.4 us (5%)
  local copies, waits for them, and re-layouts  11 us (3%)
    all_gather x1, waiting for transfers between devices, shards(): down_whole = lax.all_gather(down_weight, ('sy', 'sx'), axis=1, tiled=True)  72.9 us
    psum x1, waiting for transfers between devices, shards(): normed_grad = lax.psum(grad_terms, 'tp')  54.4 us
    psum x1, blocking collectives, global_vector(): return lax.psum(placed, ('sy', 'sx', 'tp'))  41.2 us
    all_gather x2, waiting for transfers between devices, all_channels(): return lax.all_gather(rows_array, 'tp', axis=1, tiled=True)  33.7 us
    convert_element_type x1, other arithmetic, shards(): convolved = (depthwise(extend(features), depth_kernel, image_rows, image_...  14.1 us
    dot_general x1, matrix products, shards(): lax.dot_general(preact_grad, up_weight, contract_last, preferred_element_...  12.4 us
    ppermute x4, starting transfers between devices, extended(): lax.ppermute(lax.slice_in_dim(block, block.shape[dim] - width, None, axis...  11.4 us
    ppermute x4, starting transfers between devices, extended(): lax.ppermute(lax.slice_in_dim(block, 0, width, axis=dim), axis, backward)  10.4 us
  transfers between devices with their start and end apart: 13, of which 11 were waited for; matrix products, arithmetic and copies ran while one was open for 12% of the time, Pallas kernels for 0%

commit v1 on v0

v1 whole, which is shorter than its diff:
```python
import jax
import jax.numpy as jnp
from jax import lax
from jax.sharding import PartitionSpec as P

KERNEL = 7
TILE = 8


root_half = 0.7071067811865476
root_two_pi_inv = 0.3989422804014327


def extended(block, sides, width):
    for axis, dim in sides:
        count = lax.axis_size(axis)
        forward = [(i, i + 1) for i in range(count - 1)]
        backward = [(target, source) for source, target in forward]
        low = lax.ppermute(
            lax.slice_in_dim(block, block.shape[dim] - width, None, axis=dim), axis, forward
        )
        high = lax.ppermute(lax.slice_in_dim(block, 0, width, axis=dim), axis, backward)
        block = jnp.concatenate([low, block, high], axis=dim)
    return block


def gelu_value(values):
    return 0.5 * values * (1.0 + jax.scipy.special.erf(values * root_half))


def gelu_slope(values):
    return (
        0.5 * (1.0 + jax.scipy.special.erf(values * root_half))
        + values * jnp.exp(-0.5 * values * values) * root_two_pi_inv
    )


def depthwise(padded, kernel, rows_out, cols_out, flipped):
    summed = jnp.zeros((rows_out, cols_out, kernel.shape[2]), jnp.float32)
    last_tap = KERNEL - 1
    for row_tap in range(KERNEL):
        for col_tap in range(KERNEL):
            row_start = last_tap - row_tap if flipped else row_tap
            col_start = last_tap - col_tap if flipped else col_tap
            window = padded[row_start : row_start + rows_out, col_start : col_start + cols_out]
            summed = summed + window.astype(jnp.float32) * kernel[row_tap, col_tap]
    return summed


MOST = 4


def extend(image):
    return extended(image, (("sy", 0), ("sx", 1)), KERNEL // 2)


def swapped(array):
    count = lax.axis_size("tp")
    return lax.ppermute(array, "tp", [(i, count - 1 - i) for i in range(count)])


def over_pixels(vector):
    return lax.psum(vector, ("sy", "sx"))


def conv_tiles(windows, kernel):
    summed = jnp.zeros((windows.shape[0], TILE, TILE, windows.shape[3]), jnp.float32)
    for row_tap in range(KERNEL):
        for col_tap in range(KERNEL):
            window = windows[:, row_tap : row_tap + TILE, col_tap : col_tap + TILE]
            summed = summed + window.astype(jnp.float32) * kernel[row_tap, col_tap]
    return summed


def shards(
    features,
    depth_kernel,
    depth_bias,
    norm_gain,
    norm_bias,
    up_weight,
    up_bias,
    response_gain,
    response_shift,
    down_weight,
    down_bias,
    tissue,
    cotangent,
):
    image_rows, image_cols, local_channels = features.shape
    tiles_y, tiles_x = tissue.shape
    tiles = tiles_y * tiles_x
    channels = up_weight.shape[0]
    hidden_total = up_weight.shape[1] * lax.axis_size("tp")
    tp_index = lax.axis_index("tp")
    first = tp_index == 0
    channel_start = tp_index * local_channels
    other_start = (1 - tp_index) * local_channels
    contract_last = (((1,), (1,)), ((), ()))
    pixels = MOST * TILE * TILE

    down_t = lax.all_gather(down_weight.T, ("sy", "sx"), axis=0, tiled=True)

    flags = tissue.reshape(-1)
    tile_ids = jnp.arange(tiles, dtype=jnp.int32)
    earlier = (tile_ids[None, :] < tile_ids[:, None]).astype(jnp.int32)
    ahead = jnp.sum(earlier * flags[None, :], axis=1)
    slot_of = jnp.where(flags > 0, ahead, jnp.sum(flags) + tile_ids - ahead)
    chosen = [jnp.sum(jnp.where(slot_of == s, tile_ids, 0)) for s in range(MOST)]
    slot_mask = jnp.stack([jnp.sum(jnp.where(slot_of == s, flags, 0)) for s in range(MOST)])
    mask_rows = jnp.repeat(slot_mask, TILE * TILE).astype(jnp.float32)

    def windows_of(image, side):
        return jnp.stack(
            [
                lax.dynamic_slice(
                    image,
                    ((t // tiles_x) * TILE, (t % tiles_x) * TILE, 0),
                    (side, side, image.shape[2]),
                )
                for t in chosen
            ]
        )

    def spread_out(rows_array):
        held = rows_array.reshape(MOST, TILE, TILE, rows_array.shape[1])
        held = jnp.concatenate([held, jnp.zeros_like(held[:1])], axis=0)
        slots = jnp.minimum(slot_of, MOST)
        rows = []
        for ty in range(tiles_y):
            row = [
                lax.dynamic_index_in_dim(held, slots[ty * tiles_x + tx], 0, keepdims=False)
                for tx in range(tiles_x)
            ]
            rows.append(jnp.concatenate(row, axis=1))
        return jnp.concatenate(rows, axis=0)

    def both_halves(own):
        other = swapped(own)
        return jnp.where(
            first,
            jnp.concatenate([own, other], axis=1),
            jnp.concatenate([other, own], axis=1),
        )

    cot_tiles = windows_of(cotangent, TILE).reshape(pixels, local_channels)
    masked_cot = (cot_tiles.astype(jnp.float32) * mask_rows[:, None]).astype(jnp.bfloat16)
    cot_wide = both_halves(masked_cot)

    convolved = conv_tiles(windows_of(extend(features), TILE + KERNEL - 1), depth_kernel)
    convolved = (convolved + depth_bias).astype(jnp.bfloat16).reshape(pixels, local_channels)
    gathered = both_halves(convolved).astype(jnp.float32)
    centre = jnp.mean(gathered, axis=1, keepdims=True)
    spread = jnp.mean(jnp.square(gathered - centre), axis=1, keepdims=True)
    inv_scale = lax.rsqrt(spread + 1e-06)
    standard = (gathered - centre) * inv_scale
    normed = (standard * norm_gain + norm_bias).astype(jnp.bfloat16)
    preact = jnp.dot(normed, up_weight, preferred_element_type=jnp.float32) + up_bias
    hidden = gelu_value(preact).astype(jnp.bfloat16)
    hidden_wide = hidden.astype(jnp.float32)
    squares = over_pixels(jnp.sum(mask_rows[:, None] * hidden_wide * hidden_wide, axis=0))
    column_norms = jnp.sqrt(squares)
    norms_here = jnp.full((8, 128), jnp.sum(column_norms))
    norm_level = (norms_here + swapped(norms_here))[0, 0] / hidden_total + 1e-06
    norm_ratio = column_norms / norm_level

    back_hidden = jnp.dot(cot_wide, down_t, preferred_element_type=jnp.float32)
    products = over_pixels(jnp.sum(back_hidden * hidden_wide, axis=0))

    response = (response_gain * hidden_wide * norm_ratio + response_shift + hidden_wide).astype(
        jnp.bfloat16
    )
    partial_out = lax.dot_general(
        response, down_t, contract_last, preferred_element_type=jnp.float32
    )
    sent_out = lax.dynamic_slice_in_dim(partial_out, other_start, local_channels, 1)
    kept_out = lax.dynamic_slice_in_dim(partial_out, channel_start, local_channels, 1)
    branch = kept_out + swapped(sent_out.astype(jnp.bfloat16)).astype(jnp.float32)

    ratio_grad = response_gain * products
    dots_here = jnp.full((8, 128), jnp.sum(ratio_grad * column_norms))
    dots = (dots_here + swapped(dots_here))[0, 0]
    norms_grad = ratio_grad / norm_level - dots / (hidden_total * norm_level * norm_level)
    hidden_grad = (
        back_hidden * (response_gain * norm_ratio + 1.0)
        + norms_grad * mask_rows[:, None] * hidden_wide / column_norms
    )
    preact_grad = (hidden_grad * gelu_slope(preact)).astype(jnp.bfloat16)
    grad_terms = lax.dot_general(
        preact_grad, up_weight, contract_last, preferred_element_type=jnp.float32
    )
    scaled_terms = grad_terms * norm_gain
    sums_here = jnp.stack(
        [jnp.sum(scaled_terms, axis=1), jnp.sum(scaled_terms * standard, axis=1)]
    )
    sums = sums_here + swapped(sums_here)
    sent_grad = lax.dynamic_slice_in_dim(scaled_terms, other_start, local_channels, 1)
    kept_grad = lax.dynamic_slice_in_dim(scaled_terms, channel_start, local_channels, 1)
    own_standard = lax.dynamic_slice_in_dim(standard, channel_start, local_channels, 1)
    scaled = kept_grad + swapped(sent_grad.astype(jnp.bfloat16)).astype(jnp.float32)
    convolved_grad = inv_scale * (
        scaled - (sums[0] / channels)[:, None] - own_standard * (sums[1] / channels)[:, None]
    )
    grad_image = spread_out(convolved_grad.astype(jnp.bfloat16))
    feature_grad = (
        cotangent.astype(jnp.float32)
        + depthwise(extend(grad_image), depth_kernel, image_rows, image_cols, True)
    ).astype(jnp.bfloat16)

    addend = spread_out(mask_rows[:, None] * (branch + down_bias))
    block_out = (features.astype(jnp.float32) + addend).astype(jnp.bfloat16)
    return (block_out, feature_grad)


def solution(mesh):
    placed = (
        P("sy", "sx", "tp"),
        P(None, None, "tp"),
        P("tp"),
        P(),
        P(),
        P(None, "tp"),
        P("tp"),
        P("tp"),
        P("tp"),
        P("tp", ("sy", "sx")),
        P("tp"),
        P("sy", "sx"),
        P("sy", "sx", "tp"),
    )
    return jax.shard_map(
        shards,
        mesh=mesh,
        in_specs=placed,
        out_specs=(P("sy", "sx", "tp"), P("sy", "sx", "tp")),
        check_vma=False,
    )
```

time: 339 us -> 236 us (0.70)
  waiting for transfers between devices: 173 us -> 43.9 us
  between operations: 15.4 us -> 37.6 us
  starting transfers between devices: 22 us -> 35.4 us
  matrix products: 40.4 us -> 29.1 us
  blocking collectives: 41.2 us -> 48 us
    all_gather x3 -> x1, waiting for transfers between devices: 107 us -> 12.2 us  [shards(): down_t = lax.all_gather(down_weight.T, ('sy', 'sx'), axis=0, tiled=True)]
    psum x1 -> x0, waiting for transfers between devices: 54.4 us -> none  [shards(): normed_grad = lax.psum(grad_terms, 'tp')]
    ppermute x0 -> x7, waiting for transfers between devices: none -> 17.4 us  [swapped(): return lax.ppermute(array, 'tp', [(i, count - 1 - i) for i in range(count)])]
    ppermute x4, starting transfers between devices: 10.4 us -> 18.3 us  [extended(): lax.ppermute(lax.slice_in_dim(block, 0, width, axis=dim), axis, backward)]
    ppermute x4, waiting for transfers between devices: 4.22 us -> 11.4 us  [extended(): lax.ppermute(lax.slice_in_dim(block, block.shape[dim] - width, None, axis...]
    ppermute x0 -> x7, starting transfers between devices: none -> 7.19 us  [swapped(): return lax.ppermute(array, 'tp', [(i, count - 1 - i) for i in range(count)])]
    psum x1, blocking collectives: 41.2 us -> 48 us  [over_pixels(): return lax.psum(vector, ('sy', 'sx'))]
    convert_element_type x5, other arithmetic: 16.9 us -> 10.5 us  [the longest x1 5.76 us: shards(): (convolved + depth_bias).astype(jnp.bfloat16)]
  transfers between devices with their start and end apart: 13 -> 16, of which waited for: 11 -> 10; matrix products, arithmetic and copies ran while one was open for 12% -> 15% of each run, Pallas kernels for 0% -> 0%
where the time goes in v1:
time: 236 us; the launch traced here: 235 us
  blocking collectives  48 us (20%)
  waiting for transfers between devices  43.9 us (19%)
  between operations  37.6 us (16%)
  starting transfers between devices  35.4 us (15%)
  other arithmetic  33.5 us (14%)
  matrix products  29.1 us (12%)
  local copies, waits for them, and re-layouts  7.66 us (3%)
    psum x1, blocking collectives, over_pixels(): return lax.psum(vector, ('sy', 'sx'))  48 us
    ppermute x4, starting transfers between devices, extended(): lax.ppermute(lax.slice_in_dim(block, 0, width, axis=dim), axis, backward)  18.3 us
    ppermute x7, waiting for transfers between devices, swapped(): return lax.ppermute(array, 'tp', [(i, count - 1 - i) for i in range(count)])  17.4 us
    convert_element_type x1, other arithmetic, shards(): feature_grad = (cotangent.astype(jnp.float32) + depthwise(extend(grad_ima...  14.9 us
    all_gather x1, waiting for transfers between devices, shards(): down_t = lax.all_gather(down_weight.T, ('sy', 'sx'), axis=0, tiled=True)  12.2 us
    ppermute x4, waiting for transfers between devices, extended(): lax.ppermute(lax.slice_in_dim(block, block.shape[dim] - width, None, axis...  11.4 us
    ppermute x4, starting transfers between devices, extended(): lax.ppermute(lax.slice_in_dim(block, block.shape[dim] - width, None, axis...  9.87 us
    dot_general x1, matrix products, shards(): back_hidden = jnp.dot(cot_wide, down_t, preferred_element_type=jnp.float32)  8.27 us
  transfers between devices with their start and end apart: 16, of which 10 were waited for; matrix products, arithmetic and copies ran while one was open for 15% of the time, Pallas kernels for 0%

profile of v1, /device:TPU:12, one launch (start us, length us, event | category | flops | bytes accessed | tf_op | source)
XLA Modules:
  0.0 235.3 jit_solution(2763965542860036640)
XLA Ops:
  7.9 1.0 fusion.105
  8.9 3.6 %collective-permute-start = (bf16[3,16,704]{2,1,0:T(8,128)(2,1)S(1)}, bf16[3,16,704]{2,1,0:T(8,128)(2,1)S(1)}, u32[]{:S(2)}, u32[]{:S(2)}) collective-permute-start(bf16[3,16,704]{2,1,0:T(8,128)(2,1)S(1)} %get-tuple-element.90), channel_id=1, source_target_pairs={{0,8},{8,16},{16,24},{1,9},{9,17},{17,25},{2,10},{10,18},{18,26},{... | collective-permute-start | bytes 202760 | tf_op jit(solution)/shard_map/ppermute | solution.py:19
  12.5 2.4 %collective-permute-start.1 = (bf16[3,16,704]{2,1,0:T(8,128)(2,1)S(1)}, bf16[3,16,704]{2,1,0:T(8,128)(2,1)S(1)}, u32[]{:S(2)}, u32[]{:S(2)}) collective-permute-start(bf16[3,16,704]{2,1,0:T(8,128)(2,1)S(1)} %get-tuple-element.89), channel_id=1, source_target_pairs={{8,0},{16,8},{24,16},{9,1},{17,9},{25,17},{10,2},{18,10},{26,18},{... | collective-permute-start | bytes 202760 | tf_op jit(solution)/shard_map/ppermute | solution.py:22
  15.9 1.3 reduce_sum.166
  28.8 2.7 %add_convert_fusion.4 = f32[4]{0:T(128)S(1)} fusion(s32[1]{0:T(128)} %bitcast.3, s32[1]{0:T(128)} %bitcast.2, s32[1]{0:T(128)} %bitcast.1, s32[1]{0:T(128)} %bitcast), kind=kLoop, calls=%fused_computation.313 | loop fusion | flops 16 | bytes 32 | tf_op jit(solution)/shard_map/convert_element_type | solution.py:111
  32.4 1.9 collective-permute-start.2
  34.3 3.6 %collective-permute-start.3 = (bf16[30,3,704]{2,1,0:T(4,128)(2,1)S(1)}, bf16[30,3,704]{2,1,0:T(4,128)(2,1)S(1)}, u32[]{:S(2)}, u32[]{:S(2)}) collective-permute-start(bf16[30,3,704]{2,1,0:T(4,128)(2,1)S(1)} %get-tuple-element.86), channel_id=1, source_target_pairs={{2,0},{4,2},{6,4},{3,1},{5,3},{7,5},{10,8},{12,10},{14,12},{11,9},... | collective-permute-start | bytes 380168 | tf_op jit(solution)/shard_map/ppermute | solution.py:22
  38.1 1.1 collective-permute-done.2
  39.2 1.8 collective-permute-done.3
  43.0 5.8 %add_convert_fusion.2 = bf16[4,8,8,704]{3,2,1,0:T(8,128)(2,1)S(1)} fusion(bf16[4,14,14,704]{3,2,1,0:T(8,128)(2,1)S(1)} %pad_maximum_fusion, f32[704]{0:T(1024)S(1)} %copy-done.4, f32[704]{0:T(1024)S(1)} %get-tuple-element.53, f32[704]{0:T(1024)S(1)} %get-tuple-element.54, f32[704]{0:T(1024)S(1)} %get-tuple-element.7, f32[704]{0:T(1024)S(1)} %get-tuple-element.8, ...), kind=kLoop, calls=%fused_computation.138 | loop fusion | flops 26673152 | bytes 18163200 | tf_op jit(solution)/shard_map/convert_element_type | solution.py:151
  48.8 1.6 collective-permute-start.4
  51.8 9.1 %collective-permute-done.4 = bf16[256,704]{1,0:T(8,128)(2,1)S(1)} collective-permute-done((bf16[256,704]{1,0:T(8,128)(2,1)S(1)}, bf16[256,704]{1,0:T(8,128)(2,1)S(1)}, u32[]{:S(2)}, u32[]{:S(2)}) %collective-permute-start.4) | collective-permute-done | bytes 360480 | tf_op jit(solution)/shard_map/ppermute | solution.py:59
  62.2 7.7 %convolution_add_fusion = f32[256,2816]{1,0:T(8,128)} fusion(bf16[1408,2816]{1,0:T(8,128)(2,1)} %param.18, f32[2816]{0:T(1024)S(1)} %copy-done.6, f32[1408]{0:T(1024)S(1)} %copy-done.8, f32[1408]{0:T(1024)S(1)} %copy-done.9, f32[256]{0:T(256)S(1)} %add_rsqrt_fusion, f32[256]{0:T(256)S(1)} %broadcast_multiply_fusion, bf16[256,704]{1,0:T(8,128)(2,1)S(1)} %bitcast.70, ...), kind=kOutput, calls=%fused_computation.47 | convolution fusion | flops 2036170752 | bytes 11558913 | tf_op jit(solution)/shard_map/dot_general | solution.py:158
  69.9 12.2 %all-gather.2.cloned.1.call-done = bf16[1408,2816]{1,0:T(8,128)(2,1)} async-done(((bf16[88,2816]{1,0:T(8,128)(2,1)}), bf16[1408,2816]{1,0:T(8,128)(2,1)}) %all-gather.2.cloned.1.call-update) | async-done | bytes 7929872 | tf_op jit(solution)/shard_map/all_gather | solution.py:102
  82.0 8.3 %fusion.10 = (f32[2816]{0:T(1024)S(1)}, f32[2816]{0:T(1024)S(1)}, bf16[256,2816]{1,0:T(8,128)(2,1)}, f32[256,2816]{1,0:T(8,128)}) fusion(f32[256]{0:T(256)S(1)} %convert_element_type.365, f32[256,2816]{1,0:T(8,128)} %convolution_add_fusion, bf16[1408,2816]{1,0:T(8,128)(2,1)} %all-gather.2.cloned.1.call-done, ...), kind=kOutput, calls=%fused_computation.58 | convolution fusion | flops 2041211392 | bytes 15883265 | tf_op jit(solution)/shard_map/dot_general | solution.py:167
  90.3 48.0 %all-reduce.2 = (f32[2816]{0:T(1024)S(1)}, f32[2816]{0:T(1024)S(1)}) all-reduce(f32[2816]{0:T(1024)S(1)} %get-tuple-element.4, f32[2816]{0:T(1024)S(1)} %get-tuple-element.5), channel_id=1, replica_groups=mesh['sy'=4,'sx'=4,'tp'=2] {'sy','sx'}, use_global_device_ids=true, to_apply=%region_16.17 | all-reduce | flops 5632 | bytes 45056 | tf_op jit(solution)/shard_map/psum | solution.py:63
  139.7 1.4 collective-permute-start.5
  156.7 1.1 collective-permute-done.8
  159.8 6.3 %fusion.16 = f32[256,1408]{1,0:T(8,128)S(1)} fusion(bf16[1408,2816]{1,0:T(8,128)(2,1)} %all-gather.2.cloned.1.call-done, bf16[256,2816]{1,0:T(8,128)(2,1)} %get-tuple-element.69, f32[2816]{0:T(1024)S(1)} %copy-done.7, f32[2816]{0:T(1024)S(1)} %get-tuple-element.68, f32[2816]{0:T(1024)S(1)} %copy-done.3), kind=kOutput, calls=%fused_computation.109 | convolution fusion | flops 2034368512 | bytes 10847232 | tf_op jit(solution)/shard_map/dot_general | solution.py:173
  167.0 6.9 %fusion.102 = (f32[256]{0:T(256)S(1)}, f32[256]{0:T(256)S(1)}, f32[256,1408]{1,0:T(8,128)S(1)}, f32[256,1408]{1,0:T(8,128)S(1)}) fusion(f32[256]{0:T(256)S(1)} %add_rsqrt_fusion, f32[256]{0:T(256)S(1)} %broadcast_multiply_fusion, bf16[256,704]{1,0:T(8,128)(2,1)S(1)} %bitcast.71, bf16[256,704]{1,0:T(8,128)(2,1)S(1)} %collective-permute-done.4, ...), kind=kOutput, calls=%fused_computation.322 | convolution fusion | flops 2047344128 | bytes 18787840 | tf_op jit(solution)/shard_map/dot_general | solution.py:189
  173.9 1.4 collective-permute-start.10
  176.2 1.4 collective-permute-done.10
  177.7 5.7 %collective-permute-done.9 = bf16[256,704]{1,0:T(8,128)(2,1)S(1)} collective-permute-done((bf16[256,704]{1,0:T(8,128)(2,1)S(1)}, bf16[256,704]{1,0:T(8,128)(2,1)S(1)}, u32[]{:S(2)}, u32[]{:S(2)}) %collective-permute-start.9) | collective-permute-done | bytes 360480 | tf_op jit(solution)/shard_map/ppermute | solution.py:59
  183.4 0.9 multiply_convert_fusion.1
  184.5 10.4 %collective-permute-start.12 = (bf16[3,16,704]{2,1,0:T(8,128)(2,1)S(1)}, bf16[3,16,704]{2,1,0:T(8,128)(2,1)S(1)}, u32[]{:S(2)}, u32[]{:S(2)}) collective-permute-start(bf16[3,16,704]{2,1,0:T(8,128)(2,1)S(1)} %fusion.93), channel_id=1, source_target_pairs={{8,0},{16,8},{24,16},{9,1},{17,9},{25,17},{10,2},{18,10},{26,18},{... | collective-permute-start | bytes 202760 | tf_op jit(solution)/shard_map/ppermute | solution.py:22
  194.9 1.9 collective-permute-start.11
  197.0 1.0 fusion.28
  197.9 3.2 %collective-permute-done.11 = bf16[3,16,704]{2,1,0:T(8,128)(2,1)S(1)} collective-permute-done((bf16[3,16,704]{2,1,0:T(8,128)(2,1)S(1)}, bf16[3,16,704]{2,1,0:T(8,128)(2,1)S(1)}, u32[]{:S(2)}, u32[]{:S(2)}) %collective-permute-start.11) | collective-permute-done | bytes 67616 | tf_op jit(solution)/shard_map/ppermute | solution.py:19
  201.4 1.9 collective-permute-start.13
  203.3 2.4 %collective-permute-start.14 = (bf16[30,3,704]{2,1,0:T(4,128)(2,1)S(1)}, bf16[30,3,704]{2,1,0:T(4,128)(2,1)S(1)}, u32[]{:S(2)}, u32[]{:S(2)}) collective-permute-start(bf16[30,3,704]{2,1,0:T(4,128)(2,1)S(1)} %get-tuple-element.84), channel_id=1, source_target_pairs={{0,2},{2,4},{4,6},{1,3},{3,5},{5,7},{8,10},{10,12},{12,14},{9,11},... | collective-permute-start | bytes 380168 | tf_op jit(solution)/shard_map/ppermute | solution.py:19
  206.4 7.1 %collective-permute-done.14 = bf16[30,3,704]{2,1,0:T(4,128)(2,1)S(1)} collective-permute-done((bf16[30,3,704]{2,1,0:T(4,128)(2,1)S(1)}, bf16[30,3,704]{2,1,0:T(4,128)(2,1)S(1)}, u32[]{:S(2)}, u32[]{:S(2)}) %collective-permute-start.14) | collective-permute-done | bytes 126752 | tf_op jit(solution)/shard_map/ppermute | solution.py:19
  213.5 14.9 %add_convert_fusion.1 = bf16[24,16,704]{2,1,0:T(8,128)(2,1)} fusion(bf16[24,16,704]{2,1,0:T(8,128)(2,1)S(1)} %copy-done.1, bf16[30,16,704]{2,1,0:T(8,128)(2,1)S(1)} %constant_dynamic-update-slice_fusion.3, bf16[30,3,704]{2,1,0:T(4,128)(2,1)S(1)} %collective-permute-done.14, bf16[30,3,704]{2,1,0:T(4,128)(2,1)S(1)} %collective-permute-done.13, ...), kind=kLoop, calls=%fused_computation.130 | loop fusion | flops 77316096 | bytes 5933312 | tf_op jit(solution)/shard_map/convert_element_type | solution.py:208
  (91 shorter events, 17.5 us)
Async XLA Ops:
  7.2 24.6 %copy-start.1 = (bf16[24,16,704]{2,1,0:T(8,128)(2,1)S(1)}, bf16[24,16,704]{2,1,0:T(8,128)(2,1)}, u32[]{:S(2)}) copy-start(bf16[24,16,704]{2,1,0:T(8,128)(2,1)} %param.25) | copy-start | bytes 1622020
  7.2 74.8 %all-gather.2.cloned.1.call-start = ((), (), s32[]{:S(2)}) async-start(), calls=%async_computation | async-start | bytes 8425472 | tf_op jit(solution)/shard_map/all_gather | solution.py:102
  7.9 23.9 %copy-start.2 = (f32[7,7,704]{2,1,0:T(8,128)S(1)}, f32[7,7,704]{2,1,0:T(8,128)}, u32[]{:S(2)}) copy-start(f32[7,7,704]{2,1,0:T(8,128)} %param.14) | copy-start | bytes 413956
  8.9 23.2 %copy-start = (bf16[24,16,704]{2,1,0:T(8,128)(2,1)S(1)}, bf16[24,16,704]{2,1,0:T(8,128)(2,1)}, u32[]{:S(2)}) copy-start(bf16[24,16,704]{2,1,0:T(8,128)(2,1)} %param.13) | copy-start | bytes 1622020
  8.9 23.2 %collective-permute-start = (bf16[3,16,704]{2,1,0:T(8,128)(2,1)S(1)}, bf16[3,16,704]{2,1,0:T(8,128)(2,1)S(1)}, u32[]{:S(2)}, u32[]{:S(2)}) collective-permute-start(bf16[3,16,704]{2,1,0:T(8,128)(2,1)S(1)} %get-tuple-element.90), channel_id=1, source_target_pairs={{0,8},{8,16},{16,24},{1,9},{9,17},{17,25},{2,10},{10,18},{18,26},{... | collective-permute-start | bytes 202760 | tf_op jit(solution)/shard_map/ppermute | solution.py:19
  12.5 19.7 %collective-permute-start.1 = (bf16[3,16,704]{2,1,0:T(8,128)(2,1)S(1)}, bf16[3,16,704]{2,1,0:T(8,128)(2,1)S(1)}, u32[]{:S(2)}, u32[]{:S(2)}) collective-permute-start(bf16[3,16,704]{2,1,0:T(8,128)(2,1)S(1)} %get-tuple-element.89), channel_id=1, source_target_pairs={{8,0},{16,8},{24,16},{9,1},{17,9},{25,17},{10,2},{18,10},{26,18},{... | collective-permute-start | bytes 202760 | tf_op jit(solution)/shard_map/ppermute | solution.py:22
  32.4 6.9 %collective-permute-start.2 = (bf16[30,3,704]{2,1,0:T(4,128)(2,1)S(1)}, bf16[30,3,704]{2,1,0:T(4,128)(2,1)S(1)}, u32[]{:S(2)}, u32[]{:S(2)}) collective-permute-start(bf16[30,3,704]{2,1,0:T(4,128)(2,1)S(1)} %get-tuple-element.85), channel_id=1, source_target_pairs={{0,2},{2,4},{4,6},{1,3},{3,5},{5,7},{8,10},{10,12},{12,14},{9,11},... | collective-permute-start | bytes 380168 | tf_op jit(solution)/shard_map/ppermute | solution.py:19
  34.3 6.7 %collective-permute-start.3 = (bf16[30,3,704]{2,1,0:T(4,128)(2,1)S(1)}, bf16[30,3,704]{2,1,0:T(4,128)(2,1)S(1)}, u32[]{:S(2)}, u32[]{:S(2)}) collective-permute-start(bf16[30,3,704]{2,1,0:T(4,128)(2,1)S(1)} %get-tuple-element.86), channel_id=1, source_target_pairs={{2,0},{4,2},{6,4},{3,1},{5,3},{7,5},{10,8},{12,10},{14,12},{11,9},... | collective-permute-start | bytes 380168 | tf_op jit(solution)/shard_map/ppermute | solution.py:22
  42.3 0.7 copy-start.4
  48.8 13.4 %copy-start.6 = (f32[2816]{0:T(1024)S(1)}, f32[2816]{0:T(1024)}, u32[]{:S(2)}) copy-start(f32[2816]{0:T(1024)} %param.19) | copy-start | bytes 33796
  48.8 13.4 %copy-start.8 = (f32[1408]{0:T(1024)S(1)}, f32[1408]{0:T(1024)}, u32[]{:S(2)}) copy-start(f32[1408]{0:T(1024)} %param.17) | copy-start | bytes 16900
  48.8 13.4 %copy-start.9 = (f32[1408]{0:T(1024)S(1)}, f32[1408]{0:T(1024)}, u32[]{:S(2)}) copy-start(f32[1408]{0:T(1024)} %param.16) | copy-start | bytes 16900
  48.8 12.1 %collective-permute-start.4 = (bf16[256,704]{1,0:T(8,128)(2,1)S(1)}, bf16[256,704]{1,0:T(8,128)(2,1)S(1)}, u32[]{:S(2)}, u32[]{:S(2)}) collective-permute-start(bf16[256,704]{1,0:T(8,128)(2,1)S(1)} %bitcast.67), channel_id=1, source_target_pairs={{0,1},{1,0},{2,3},{3,2},{4,5},{5,4},{6,7},{7,6},{8,9},{9,8},{10,11... | collective-permute-start | bytes 1081352 | tf_op jit(solution)/shard_map/ppermute | solution.py:59
  50.5 19.3 %collective-permute-start.7 = (bf16[256,704]{1,0:T(8,128)(2,1)S(1)}, bf16[256,704]{1,0:T(8,128)(2,1)S(1)}, u32[]{:S(2)}, u32[]{:S(2)}) collective-permute-start(bf16[256,704]{1,0:T(8,128)(2,1)S(1)} %fusion.29), channel_id=1, source_target_pairs={{0,1},{1,0},{2,3},{3,2},{4,5},{5,4},{6,7},{7,6},{8,9},{9,8},{10,11... | collective-permute-start | bytes 1081352 | tf_op jit(solution)/shard_map/ppermute | solution.py:59
  69.8 68.5 %copy-start.3 = (f32[2816]{0:T(1024)S(1)}, f32[2816]{0:T(1024)}, u32[]{:S(2)}) copy-start(f32[2816]{0:T(1024)} %param.20) | copy-start | bytes 33796
  69.8 89.9 %copy-start.7 = (f32[2816]{0:T(1024)S(1)}, f32[2816]{0:T(1024)}, u32[]{:S(2)}) copy-start(f32[2816]{0:T(1024)} %param.21) | copy-start | bytes 33796
  139.7 15.2 %collective-permute-start.5 = (f32[8,128]{1,0:T(8,128)S(1)}, f32[8,128]{1,0:T(8,128)S(1)}, u32[]{:S(2)}, u32[]{:S(2)}) collective-permute-start(f32[8,128]{1,0:T(8,128)S(1)} %broadcast_in_dim.16), channel_id=1, source_target_pairs={{0,1},{1,0},{2,3},{3,2},{4,5},{5,4},{6,7},{7,6},{8,9},{9,8},{10,11... | collective-permute-start | bytes 12296 | tf_op jit(solution)/shard_map/ppermute | solution.py:59
  154.2 3.7 %collective-permute-start.8 = (f32[8,128]{1,0:T(8,128)S(1)}, f32[8,128]{1,0:T(8,128)S(1)}, u32[]{:S(2)}, u32[]{:S(2)}) collective-permute-start(f32[8,128]{1,0:T(8,128)S(1)} %broadcast_in_dim.17), channel_id=1, source_target_pairs={{0,1},{1,0},{2,3},{3,2},{4,5},{5,4},{6,7},{7,6},{8,9},{9,8},{10,11... | collective-permute-start | bytes 12296 | tf_op jit(solution)/shard_map/ppermute | solution.py:59
  159.7 7.2 %copy-start.10 = (f32[256,2816]{1,0:T(8,128)S(1)}, f32[256,2816]{1,0:T(8,128)}, u32[]{:S(2)}) copy-start(f32[256,2816]{1,0:T(8,128)} %convolution_add_fusion) | copy-start | bytes 8650756
  159.8 7.2 %copy-start.11 = (f32[256,2816]{1,0:T(8,128)S(1)}, f32[256,2816]{1,0:T(8,128)}, u32[]{:S(2)}) copy-start(f32[256,2816]{1,0:T(8,128)} %get-tuple-element.114) | copy-start | bytes 8650756
  159.8 7.2 %copy-start.12 = (bf16[256,2816]{1,0:T(8,128)(2,1)S(1)}, bf16[256,2816]{1,0:T(8,128)(2,1)}, u32[]{:S(2)}) copy-start(bf16[256,2816]{1,0:T(8,128)(2,1)} %get-tuple-element.69) | copy-start | bytes 4325380
  166.2 11.4 %collective-permute-start.6 = (bf16[256,704]{1,0:T(8,128)(2,1)S(1)}, bf16[256,704]{1,0:T(8,128)(2,1)S(1)}, u32[]{:S(2)}, u32[]{:S(2)}) collective-permute-start(bf16[256,704]{1,0:T(8,128)(2,1)S(1)} %dynamic-slice_convert_fusion.1), channel_id=1, source_target_pairs={{0,1},{1,0},{2,3},{3,2},{4,5},{5,4},{6,7},{7,6},{8,9},{9,8},{10,11... | collective-permute-start | bytes 1081352 | tf_op jit(solution)/shard_map/ppermute | solution.py:59
  167.0 16.4 %copy-start.5 = (f32[704]{0:T(1024)S(1)}, f32[704]{0:T(1024)}, u32[]{:S(2)}) copy-start(f32[704]{0:T(1024)} %param.23) | copy-start | bytes 8452
  173.9 3.7 %collective-permute-start.10 = (f32[2,256]{1,0:T(2,128)S(1)}, f32[2,256]{1,0:T(2,128)S(1)}, u32[]{:S(2)}, u32[]{:S(2)}) collective-permute-start(f32[2,256]{1,0:T(2,128)S(1)} %pad_maximum_fusion.8), channel_id=1, source_target_pairs={{0,1},{1,0},{2,3},{3,2},{4,5},{5,4},{6,7},{7,6},{8,9},{9,8},{10,11... | collective-permute-start | bytes 6152 | tf_op jit(solution)/shard_map/ppermute | solution.py:59
  175.5 7.8 %collective-permute-start.9 = (bf16[256,704]{1,0:T(8,128)(2,1)S(1)}, bf16[256,704]{1,0:T(8,128)(2,1)S(1)}, u32[]{:S(2)}, u32[]{:S(2)}) collective-permute-start(bf16[256,704]{1,0:T(8,128)(2,1)S(1)} %dynamic-slice_convert_fusion), channel_id=1, source_target_pairs={{0,1},{1,0},{2,3},{3,2},{4,5},{5,4},{6,7},{7,6},{8,9},{9,8},{10,11... | collective-permute-start | bytes 1081352 | tf_op jit(solution)/shard_map/ppermute | solution.py:59
  184.5 16.8 %collective-permute-start.12 = (bf16[3,16,704]{2,1,0:T(8,128)(2,1)S(1)}, bf16[3,16,704]{2,1,0:T(8,128)(2,1)S(1)}, u32[]{:S(2)}, u32[]{:S(2)}) collective-permute-start(bf16[3,16,704]{2,1,0:T(8,128)(2,1)S(1)} %fusion.93), channel_id=1, source_target_pairs={{8,0},{16,8},{24,16},{9,1},{17,9},{25,17},{10,2},{18,10},{26,18},{... | collective-permute-start | bytes 202760 | tf_op jit(solution)/shard_map/ppermute | solution.py:22
  194.9 6.2 %collective-permute-start.11 = (bf16[3,16,704]{2,1,0:T(8,128)(2,1)S(1)}, bf16[3,16,704]{2,1,0:T(8,128)(2,1)S(1)}, u32[]{:S(2)}, u32[]{:S(2)}) collective-permute-start(bf16[3,16,704]{2,1,0:T(8,128)(2,1)S(1)} %fusion.94), channel_id=1, source_target_pairs={{0,8},{8,16},{16,24},{1,9},{9,17},{17,25},{2,10},{10,18},{18,26},{... | collective-permute-start | bytes 202760 | tf_op jit(solution)/shard_map/ppermute | solution.py:19
  201.4 5.0 %collective-permute-start.13 = (bf16[30,3,704]{2,1,0:T(4,128)(2,1)S(1)}, bf16[30,3,704]{2,1,0:T(4,128)(2,1)S(1)}, u32[]{:S(2)}, u32[]{:S(2)}) collective-permute-start(bf16[30,3,704]{2,1,0:T(4,128)(2,1)S(1)} %get-tuple-element.83), channel_id=1, source_target_pairs={{2,0},{4,2},{6,4},{3,1},{5,3},{7,5},{10,8},{12,10},{14,12},{11,9},... | collective-permute-start | bytes 380168 | tf_op jit(solution)/shard_map/ppermute | solution.py:22
  203.3 10.2 %collective-permute-start.14 = (bf16[30,3,704]{2,1,0:T(4,128)(2,1)S(1)}, bf16[30,3,704]{2,1,0:T(4,128)(2,1)S(1)}, u32[]{:S(2)}, u32[]{:S(2)}) collective-permute-start(bf16[30,3,704]{2,1,0:T(4,128)(2,1)S(1)} %get-tuple-element.84), channel_id=1, source_target_pairs={{0,2},{2,4},{4,6},{1,3},{3,5},{5,7},{8,10},{10,12},{12,14},{9,11},... | collective-permute-start | bytes 380168 | tf_op jit(solution)/shard_map/ppermute | solution.py:19
Sparse Core Ops, SparseCore 0:
  10.2 71.7 all-gather.1

commit v2 on v1

--- a/solution.py
+++ b/solution.py
@@ -1,6 +1,10 @@
+import functools
+
 import jax
 import jax.numpy as jnp
 from jax import lax
+from jax.experimental import pallas as pl
+from jax.experimental.pallas import tpu as pltpu
 from jax.sharding import PartitionSpec as P
 
 KERNEL = 7
@@ -59,10 +63,6 @@
     return lax.ppermute(array, "tp", [(i, count - 1 - i) for i in range(count)])
 
 
-def over_pixels(vector):
-    return lax.psum(vector, ("sy", "sx"))
-
-
 def conv_tiles(windows, kernel):
     summed = jnp.zeros((windows.shape[0], TILE, TILE, windows.shape[3]), jnp.float32)
     for row_tap in range(KERNEL):
@@ -70,6 +70,119 @@
             window = windows[:, row_tap : row_tap + TILE, col_tap : col_tap + TILE]
             summed = summed + window.astype(jnp.float32) * kernel[row_tap, col_tap]
     return summed
+
+
+MESH = pl.DeviceIdType.MESH
+
+
+def peers_of(axis, count):
+    me = lax.axis_index(axis)
+    return [lax.rem(me + step, count) for step in range(1, count)]
+
+
+def send_round(source, slots, axis, peers, send_sems, recv_sems):
+    copies = []
+    for step, peer in enumerate(peers):
+        copy = pltpu.make_async_remote_copy(
+            src_ref=source,
+            dst_ref=slots.at[step],
+            send_sem=send_sems.at[step],
+            recv_sem=recv_sems.at[step],
+            device_id={axis: peer},
+            device_id_type=MESH,
+        )
+        copy.start()
+        copies.append(copy)
+    return copies
+
+
+def sums_kernel(
+    sx_count,
+    sy_count,
+    vector_ref,
+    gain_ref,
+    scale_ref,
+    slope_ref,
+    sx_slots,
+    total,
+    sy_slots,
+    pair,
+    pair_slot,
+    sx_send,
+    sx_recv,
+    sy_send,
+    sy_recv,
+    tp_send,
+    tp_recv,
+):
+    width = gain_ref.shape[1]
+    units = 2 * width
+    sx_peers = peers_of("sx", sx_count)
+    sy_peers = peers_of("sy", sy_count)
+    tp_peer = 1 - lax.axis_index("tp")
+    barrier = pltpu.get_barrier_semaphore()
+    for axis, peers in (("sx", sx_peers), ("sy", sy_peers), ("tp", [tp_peer])):
+        for peer in peers:
+            pl.semaphore_signal(barrier, inc=1, device_id={axis: peer}, device_id_type=MESH)
+    pl.semaphore_wait(barrier, len(sx_peers) + len(sy_peers) + 1)
+
+    copies = send_round(vector_ref, sx_slots, "sx", sx_peers, sx_send, sx_recv)
+    summed = vector_ref[...]
+    for step, copy in enumerate(copies):
+        copy.wait()
+        summed = summed + sx_slots[step]
+    total[...] = summed
+    copies = send_round(total, sy_slots, "sy", sy_peers, sy_send, sy_recv)
+    for step, copy in enumerate(copies):
+        copy.wait()
+        summed = summed + sy_slots[step]
+    norms = jnp.sqrt(summed[:, :width])
+    ratio_grad = gain_ref[...] * summed[:, width:]
+    norms_sum = jnp.sum(norms, axis=1, keepdims=True)
+    dots_sum = jnp.sum(ratio_grad * norms, axis=1, keepdims=True)
+    pair[:, :128] = jnp.broadcast_to(norms_sum, (1, 128))
+    pair[:, 128:] = jnp.broadcast_to(dots_sum, (1, 128))
+    copy = pltpu.make_async_remote_copy(
+        src_ref=pair,
+        dst_ref=pair_slot,
+        send_sem=tp_send,
+        recv_sem=tp_recv,
+        device_id={"tp": tp_peer},
+        device_id_type=MESH,
+    )
+    copy.start()
+    copy.wait()
+    level = (pair[:, :1] + pair_slot[:, :1]) / units + 1e-06
+    dots = pair[:, 128:129] + pair_slot[:, 128:129]
+    scale_ref[...] = gain_ref[...] * (norms / level) + 1.0
+    slope_ref[...] = (ratio_grad / level - dots / (units * level * level)) / norms
+
+
+def response_scales(squares, products, gain):
+    width = gain.shape[0]
+    sx_count = lax.axis_size("sx")
+    sy_count = lax.axis_size("sy")
+    scale, slope = pl.pallas_call(
+        functools.partial(sums_kernel, sx_count, sy_count),
+        out_shape=[jax.ShapeDtypeStruct((1, width), jnp.float32)] * 2,
+        in_specs=[pl.BlockSpec(memory_space=pltpu.VMEM)] * 2,
+        out_specs=[pl.BlockSpec(memory_space=pltpu.VMEM)] * 2,
+        scratch_shapes=[
+            pltpu.VMEM((sx_count - 1, 1, 2 * width), jnp.float32),
+            pltpu.VMEM((1, 2 * width), jnp.float32),
+            pltpu.VMEM((sy_count - 1, 1, 2 * width), jnp.float32),
+            pltpu.VMEM((1, 256), jnp.float32),
+            pltpu.VMEM((1, 256), jnp.float32),
+            pltpu.SemaphoreType.DMA((sx_count - 1,)),
+            pltpu.SemaphoreType.DMA((sx_count - 1,)),
+            pltpu.SemaphoreType.DMA((sy_count - 1,)),
+            pltpu.SemaphoreType.DMA((sy_count - 1,)),
+            pltpu.SemaphoreType.DMA,
+            pltpu.SemaphoreType.DMA,
+        ],
+        compiler_params=pltpu.CompilerParams(collective_id=0, has_side_effects=True),
+    )(jnp.concatenate([squares, products])[None], gain[None])
+    return scale, slope
 
 
 def shards(
@@ -91,7 +204,6 @@
     tiles_y, tiles_x = tissue.shape
     tiles = tiles_y * tiles_x
     channels = up_weight.shape[0]
-    hidden_total = up_weight.shape[1] * lax.axis_size("tp")
     tp_index = lax.axis_index("tp")
     first = tp_index == 0
     channel_start = tp_index * local_channels
@@ -158,18 +270,13 @@
     preact = jnp.dot(normed, up_weight, preferred_element_type=jnp.float32) + up_bias
     hidden = gelu_value(preact).astype(jnp.bfloat16)
     hidden_wide = hidden.astype(jnp.float32)
-    squares = over_pixels(jnp.sum(mask_rows[:, None] * hidden_wide * hidden_wide, axis=0))
-    column_norms = jnp.sqrt(squares)
-    norms_here = jnp.full((8, 128), jnp.sum(column_norms))
-    norm_level = (norms_here + swapped(norms_here))[0, 0] / hidden_total + 1e-06
-    norm_ratio = column_norms / norm_level
+    squares = jnp.sum(mask_rows[:, None] * hidden_wide * hidden_wide, axis=0)
 
     back_hidden = jnp.dot(cot_wide, down_t, preferred_element_type=jnp.float32)
-    products = over_pixels(jnp.sum(back_hidden * hidden_wide, axis=0))
-
-    response = (response_gain * hidden_wide * norm_ratio + response_shift + hidden_wide).astype(
-        jnp.bfloat16
-    )
+    products = jnp.sum(back_hidden * hidden_wide, axis=0)
+    scale, slope = response_scales(squares, products, response_gain)
+
+    response = (hidden_wide * scale + response_shift).astype(jnp.bfloat16)
     partial_out = lax.dot_general(
         response, down_t, contract_last, preferred_element_type=jnp.float32
     )
@@ -177,14 +284,7 @@
     kept_out = lax.dynamic_slice_in_dim(partial_out, channel_start, local_channels, 1)
     branch = kept_out + swapped(sent_out.astype(jnp.bfloat16)).astype(jnp.float32)
 
-    ratio_grad = response_gain * products
-    dots_here = jnp.full((8, 128), jnp.sum(ratio_grad * column_norms))
-    dots = (dots_here + swapped(dots_here))[0, 0]
-    norms_grad = ratio_grad / norm_level - dots / (hidden_total * norm_level * norm_level)
-    hidden_grad = (
-        back_hidden * (response_gain * norm_ratio + 1.0)
-        + norms_grad * mask_rows[:, None] * hidden_wide / column_norms
-    )
+    hidden_grad = back_hidden * scale + slope * mask_rows[:, None] * hidden_wide
     preact_grad = (hidden_grad * gelu_slope(preact)).astype(jnp.bfloat16)
     grad_terms = lax.dot_general(
         preact_grad, up_weight, contract_last, preferred_element_type=jnp.float32

time: 236 us -> 179 us (0.76)
  blocking collectives: 48 us -> 0 us
  waiting for transfers between devices: 43.9 us -> 26.4 us
  Pallas kernels: 0 us -> 13.4 us
  starting transfers between devices: 35.4 us -> 26.7 us
  matrix products: 29.1 us -> 32.3 us
    psum x1 -> x0, blocking collectives: 48 us -> none  [over_pixels(): return lax.psum(vector, ('sy', 'sx'))]
    pallas_call x0 -> x1, Pallas kernels: none -> 13.4 us  [response_scales(): pl.pallas_call(functools.partial(sums_kernel, sx_count, sy_count), out_sh...]
    ppermute x7 -> x5, waiting for transfers between devices: 17.4 us -> 8.11 us  [swapped(): return lax.ppermute(array, 'tp', [(i, count - 1 - i) for i in range(count)])]
    ppermute x4, starting transfers between devices: 18.3 us -> 11 us  [extended(): lax.ppermute(lax.slice_in_dim(block, 0, width, axis=dim), axis, backward)]
    ppermute x4, waiting for transfers between devices: 11.4 us -> 7.2 us  [extended(): lax.ppermute(lax.slice_in_dim(block, block.shape[dim] - width, None, axis...]
    all_gather x1, waiting for transfers between devices: 12.2 us -> 8.18 us  [shards(): down_t = lax.all_gather(down_weight.T, ('sy', 'sx'), axis=0, tiled=True)]
    dot_general x1, matrix products: 6.92 us -> 9.93 us  [shards(): lax.dot_general(preact_grad, up_weight, contract_last, preferred_element_...]
    pallas_call x0 -> x2, other arithmetic: none -> 2.66 us  [response_scales(): pl.pallas_call(functools.partial(sums_kernel, sx_count, sy_count), out_sh...]
  transfers between devices with their start and end apart: 16 -> 14, of which waited for: 10 -> 8; matrix products, arithmetic and copies ran while one was open for 15% -> 22% of each run, Pallas kernels for 0% -> 0%
where the time goes in v2:
time: 179 us; the launch traced here: 178 us
  between operations  36.5 us (20%)
  other arithmetic  35.2 us (20%)
  matrix products  32.3 us (18%)
  starting transfers between devices  26.7 us (15%)
  waiting for transfers between devices  26.4 us (15%)
  Pallas kernels  13.4 us (7%)
  local copies, waits for them, and re-layouts  7.28 us (4%)
    convert_element_type x1, other arithmetic, shards(): feature_grad = (cotangent.astype(jnp.float32) + depthwise(extend(grad_ima...  15.1 us
    pallas_call x1, Pallas kernels, response_scales(): pl.pallas_call(functools.partial(sums_kernel, sx_count, sy_count), out_sh...  13.4 us
    ppermute x4, starting transfers between devices, extended(): lax.ppermute(lax.slice_in_dim(block, 0, width, axis=dim), axis, backward)  11 us
    ppermute x4, starting transfers between devices, extended(): lax.ppermute(lax.slice_in_dim(block, block.shape[dim] - width, None, axis...  10.7 us
    dot_general x1, matrix products, shards(): lax.dot_general(preact_grad, up_weight, contract_last, preferred_element_...  9.93 us
    dot_general x1, matrix products, shards(): back_hidden = jnp.dot(cot_wide, down_t, preferred_element_type=jnp.float32)  8.26 us
    all_gather x1, waiting for transfers between devices, shards(): down_t = lax.all_gather(down_weight.T, ('sy', 'sx'), axis=0, tiled=True)  8.18 us
    ppermute x5, waiting for transfers between devices, swapped(): return lax.ppermute(array, 'tp', [(i, count - 1 - i) for i in range(count)])  8.11 us
  transfers between devices with their start and end apart: 14, of which 8 were waited for; matrix products, arithmetic and copies ran while one was open for 22% of the time, Pallas kernels for 0%

profile of v2, /device:TPU:12, one launch (start us, length us, event | category | flops | bytes accessed | tf_op | source)
XLA Modules:
  0.0 177.9 jit_solution(17822429870710681256)
XLA Ops:
  7.9 1.0 fusion.102
  8.9 3.6 %collective-permute-start = (bf16[3,16,704]{2,1,0:T(8,128)(2,1)S(1)}, bf16[3,16,704]{2,1,0:T(8,128)(2,1)S(1)}, u32[]{:S(2)}, u32[]{:S(2)}) collective-permute-start(bf16[3,16,704]{2,1,0:T(8,128)(2,1)S(1)} %get-tuple-element.88), channel_id=1, source_target_pairs={{0,8},{8,16},{16,24},{1,9},{9,17},{17,25},{2,10},{10,18},{18,26},{... | collective-permute-start | bytes 202760 | tf_op jit(solution)/shard_map/ppermute | solution.py:23
  12.5 2.4 %collective-permute-start.1 = (bf16[3,16,704]{2,1,0:T(8,128)(2,1)S(1)}, bf16[3,16,704]{2,1,0:T(8,128)(2,1)S(1)}, u32[]{:S(2)}, u32[]{:S(2)}) collective-permute-start(bf16[3,16,704]{2,1,0:T(8,128)(2,1)S(1)} %get-tuple-element.87), channel_id=1, source_target_pairs={{8,0},{16,8},{24,16},{9,1},{17,9},{25,17},{10,2},{18,10},{26,18},{... | collective-permute-start | bytes 202760 | tf_op jit(solution)/shard_map/ppermute | solution.py:26
  15.9 1.3 reduce_sum.148
  28.8 2.7 %add_convert_fusion.4 = f32[4]{0:T(128)S(1)} fusion(s32[1]{0:T(128)} %bitcast.3, s32[1]{0:T(128)} %bitcast.2, s32[1]{0:T(128)} %bitcast.1, s32[1]{0:T(128)} %bitcast), kind=kLoop, calls=%fused_computation.304 | loop fusion | flops 16 | bytes 32 | tf_op jit(solution)/shard_map/convert_element_type | solution.py:223
  32.4 1.9 %collective-permute-start.2 = (bf16[30,3,704]{2,1,0:T(4,128)(2,1)S(1)}, bf16[30,3,704]{2,1,0:T(4,128)(2,1)S(1)}, u32[]{:S(2)}, u32[]{:S(2)}) collective-permute-start(bf16[30,3,704]{2,1,0:T(4,128)(2,1)S(1)} %get-tuple-element.83), channel_id=1, source_target_pairs={{0,2},{2,4},{4,6},{1,3},{3,5},{5,7},{8,10},{10,12},{12,14},{9,11},... | collective-permute-start | bytes 380168 | tf_op jit(solution)/shard_map/ppermute | solution.py:23
  34.3 3.6 %collective-permute-start.3 = (bf16[30,3,704]{2,1,0:T(4,128)(2,1)S(1)}, bf16[30,3,704]{2,1,0:T(4,128)(2,1)S(1)}, u32[]{:S(2)}, u32[]{:S(2)}) collective-permute-start(bf16[30,3,704]{2,1,0:T(4,128)(2,1)S(1)} %get-tuple-element.84), channel_id=1, source_target_pairs={{2,0},{4,2},{6,4},{3,1},{5,3},{7,5},{10,8},{12,10},{14,12},{11,9},... | collective-permute-start | bytes 380168 | tf_op jit(solution)/shard_map/ppermute | solution.py:26
  38.3 1.0 collective-permute-done.2
  39.2 1.8 collective-permute-done.3
  43.0 5.8 %add_convert_fusion.2 = bf16[4,8,8,704]{3,2,1,0:T(8,128)(2,1)S(1)} fusion(bf16[4,14,14,704]{3,2,1,0:T(8,128)(2,1)S(1)} %pad_maximum_fusion, f32[704]{0:T(1024)S(1)} %copy-done.32, f32[704]{0:T(1024)S(1)} %get-tuple-element.57, f32[704]{0:T(1024)S(1)} %get-tuple-element.58, f32[704]{0:T(1024)S(1)} %get-tuple-element.11, f32[704]{0:T(1024)S(1)} %get-tuple-element.12, ...), kind=kLoop, calls=%fused_computation.134 | loop fusion | flops 26673152 | bytes 18163200 | tf_op jit(solution)/shard_map/convert_element_type | solution.py:263
  48.8 1.6 collective-permute-start.4
  65.8 8.0 %convolution_add_fusion = f32[256,2816]{1,0:T(8,128)} fusion(bf16[1408,2816]{1,0:T(8,128)(2,1)} %param.18, f32[2816]{0:T(1024)S(1)} %copy-done.37, f32[1408]{0:T(1024)S(1)} %copy-done.38, f32[1408]{0:T(1024)S(1)} %copy-done.39, f32[256]{0:T(256)S(1)} %add_rsqrt_fusion, f32[256]{0:T(256)S(1)} %broadcast_multiply_fusion, bf16[256,704]{1,0:T(8,128)(2,1)S(1)} %bitcast.68, ...), kind=kOutput, calls=%fused_computation.46 | convolution fusion | flops 2036170752 | bytes 11558913 | tf_op jit(solution)/shard_map/dot_general | solution.py:270
  73.8 8.2 %all-gather.2.cloned.1.call-done = bf16[1408,2816]{1,0:T(8,128)(2,1)} async-done(((bf16[88,2816]{1,0:T(8,128)(2,1)}), bf16[1408,2816]{1,0:T(8,128)(2,1)}) %all-gather.2.cloned.1.call-update) | async-done | bytes 7929872 | tf_op jit(solution)/shard_map/all_gather | solution.py:214
  82.0 8.3 %fusion.6 = (f32[2816]{0:T(1024)S(1)}, f32[2816]{0:T(1024)S(1)}, bf16[256,2816]{1,0:T(8,128)(2,1)}, f32[256,2816]{1,0:T(8,128)}) fusion(f32[256]{0:T(256)S(1)} %convert_element_type.365, f32[256,2816]{1,0:T(8,128)} %convolution_add_fusion, bf16[1408,2816]{1,0:T(8,128)(2,1)} %all-gather.2.cloned.1.call-done, ...), kind=kOutput, calls=%fused_computation.53 | convolution fusion | flops 2041211392 | bytes 15883265 | tf_op jit(solution)/shard_map/dot_general | solution.py:275
  90.9 13.4 %shard_map.140 = (f32[1,2816]{1,0:T(1,128)}, f32[1,2816]{1,0:T(1,128)}) custom-call(f32[1,5632]{1,0:T(1,128)} %broadcast_in_dim.16.vector_ref, f32[1,2816]{1,0:T(1,128)} %broadcast_in_dim.17.gain_ref), custom_call_target="tpu_custom_call" | custom-call | tf_op jit(solution)/shard_map/pallas_call | solution.py:165
  104.3 1.3 reduce.58
  105.7 6.1 %fusion.14 = f32[256,1408]{1,0:T(8,128)S(1)} fusion(bf16[1408,2816]{1,0:T(8,128)(2,1)} %all-gather.2.cloned.1.call-done, bf16[256,2816]{1,0:T(8,128)(2,1)} %get-tuple-element.67, f32[2816]{0:T(1024)} %param.21, f32[2816]{0:T(1024)} %reduce.58), kind=kOutput, calls=%fused_computation.106 | convolution fusion | flops 2032926720 | bytes 10835968 | tf_op jit(solution)/shard_map/dot_general | solution.py:280
  111.8 0.9 dynamic-slice_convert_fusion.1
  113.4 1.3 reduce.59
  114.8 9.9 %fusion.99 = (f32[256]{0:T(256)S(1)}, f32[256]{0:T(256)S(1)}, f32[256,1408]{1,0:T(8,128)S(1)}, f32[256,1408]{1,0:T(8,128)S(1)}) fusion(f32[256]{0:T(256)} %copy-done.34, f32[256]{0:T(256)} %copy-done.36, bf16[256,704]{1,0:T(8,128)(2,1)S(1)} %bitcast.69, bf16[256,704]{1,0:T(8,128)(2,1)S(1)} %collective-permute-done.4, pred[]{:T(512)S(6)} %eq.40, ...), kind=kOutput, calls=%fused_computation.312 | convolution fusion | flops 2046623232 | bytes 18776576 | tf_op jit(solution)/shard_map/dot_general | solution.py:289
  124.7 1.4 collective-permute-start.8
  127.1 1.4 collective-permute-done.8
  128.5 6.7 %collective-permute-done.7 = bf16[256,704]{1,0:T(8,128)(2,1)S(1)} collective-permute-done((bf16[256,704]{1,0:T(8,128)(2,1)S(1)}, bf16[256,704]{1,0:T(8,128)(2,1)S(1)}, u32[]{:S(2)}, u32[]{:S(2)}) %collective-permute-start.7) | collective-permute-done | bytes 360480 | tf_op jit(solution)/shard_map/ppermute | solution.py:63
  135.2 1.9 %multiply_convert_fusion.1 = (bf16[256,704]{1,0:T(8,128)(2,1)S(1)}, f32[256,704]{1,0:T(8,128)S(1)}) fusion(f32[256,1408]{1,0:T(8,128)S(1)} %get-tuple-element.74, s32[]{:T(128)S(6)} %select_n.222, bf16[256,704]{1,0:T(8,128)(2,1)S(1)} %collective-permute-done.7, f32[256,1408]{1,0:T(8,128)S(1)} %get-tuple-element.111, f32[256]{0:T(256)S(1)} %bitcast.74, ...), kind=kLoop, calls=%fused_computation.130 | loop fusion | flops 1982464 | bytes 3971844 | tf_op jit(solution)/shard_map/convert_element_type | solution.py:304
  137.3 3.1 %collective-permute-start.10 = (bf16[3,16,704]{2,1,0:T(8,128)(2,1)S(1)}, bf16[3,16,704]{2,1,0:T(8,128)(2,1)S(1)}, u32[]{:S(2)}, u32[]{:S(2)}) collective-permute-start(bf16[3,16,704]{2,1,0:T(8,128)(2,1)S(1)} %fusion.90), channel_id=1, source_target_pairs={{8,0},{16,8},{24,16},{9,1},{17,9},{25,17},{10,2},{18,10},{26,18},{... | collective-permute-start | bytes 202760 | tf_op jit(solution)/shard_map/ppermute | solution.py:26
  140.4 2.7 %collective-permute-start.9 = (bf16[3,16,704]{2,1,0:T(8,128)(2,1)S(1)}, bf16[3,16,704]{2,1,0:T(8,128)(2,1)S(1)}, u32[]{:S(2)}, u32[]{:S(2)}) collective-permute-start(bf16[3,16,704]{2,1,0:T(8,128)(2,1)S(1)} %fusion.91), channel_id=1, source_target_pairs={{0,8},{8,16},{16,24},{1,9},{9,17},{17,25},{2,10},{10,18},{18,26},{... | collective-permute-start | bytes 202760 | tf_op jit(solution)/shard_map/ppermute | solution.py:23
  143.3 1.0 fusion.25
  144.3 2.4 %collective-permute-done.9 = bf16[3,16,704]{2,1,0:T(8,128)(2,1)S(1)} collective-permute-done((bf16[3,16,704]{2,1,0:T(8,128)(2,1)S(1)}, bf16[3,16,704]{2,1,0:T(8,128)(2,1)S(1)}, u32[]{:S(2)}, u32[]{:S(2)}) %collective-permute-start.9) | collective-permute-done | bytes 67616 | tf_op jit(solution)/shard_map/ppermute | solution.py:23
  147.1 1.9 %collective-permute-start.11 = (bf16[30,3,704]{2,1,0:T(4,128)(2,1)S(1)}, bf16[30,3,704]{2,1,0:T(4,128)(2,1)S(1)}, u32[]{:S(2)}, u32[]{:S(2)}) collective-permute-start(bf16[30,3,704]{2,1,0:T(4,128)(2,1)S(1)} %get-tuple-element.81), channel_id=1, source_target_pairs={{2,0},{4,2},{6,4},{3,1},{5,3},{7,5},{10,8},{12,10},{14,12},{11,9},... | collective-permute-start | bytes 380168 | tf_op jit(solution)/shard_map/ppermute | solution.py:26
  149.0 2.4 %collective-permute-start.12 = (bf16[30,3,704]{2,1,0:T(4,128)(2,1)S(1)}, bf16[30,3,704]{2,1,0:T(4,128)(2,1)S(1)}, u32[]{:S(2)}, u32[]{:S(2)}) collective-permute-start(bf16[30,3,704]{2,1,0:T(4,128)(2,1)S(1)} %get-tuple-element.82), channel_id=1, source_target_pairs={{0,2},{2,4},{4,6},{1,3},{3,5},{5,7},{8,10},{10,12},{12,14},{9,11},... | collective-permute-start | bytes 380168 | tf_op jit(solution)/shard_map/ppermute | solution.py:23
  152.0 3.8 %collective-permute-done.12 = bf16[30,3,704]{2,1,0:T(4,128)(2,1)S(1)} collective-permute-done((bf16[30,3,704]{2,1,0:T(4,128)(2,1)S(1)}, bf16[30,3,704]{2,1,0:T(4,128)(2,1)S(1)}, u32[]{:S(2)}, u32[]{:S(2)}) %collective-permute-start.12) | collective-permute-done | bytes 126752 | tf_op jit(solution)/shard_map/ppermute | solution.py:23
  156.0 15.1 %add_convert_fusion.1 = bf16[24,16,704]{2,1,0:T(8,128)(2,1)} fusion(bf16[24,16,704]{2,1,0:T(8,128)(2,1)S(1)} %copy-done.1, bf16[30,16,704]{2,1,0:T(8,128)(2,1)S(1)} %constant_dynamic-update-slice_fusion.3, bf16[30,3,704]{2,1,0:T(4,128)(2,1)S(1)} %collective-permute-done.12, bf16[30,3,704]{2,1,0:T(4,128)(2,1)S(1)} %collective-permute-done.11, ...), kind=kLoop, calls=%fused_computation.126 | loop fusion | flops 77316096 | bytes 5933312 | tf_op jit(solution)/shard_map/convert_element_type | solution.py:308
  (138 shorter events, 13.5 us)
Async XLA Ops:
  7.2 24.6 %copy-start.1 = (bf16[24,16,704]{2,1,0:T(8,128)(2,1)S(1)}, bf16[24,16,704]{2,1,0:T(8,128)(2,1)}, u32[]{:S(2)}) copy-start(bf16[24,16,704]{2,1,0:T(8,128)(2,1)} %param.25) | copy-start | bytes 1622020
  7.2 74.8 %all-gather.2.cloned.1.call-start = ((), (), s32[]{:S(2)}) async-start(), calls=%async_computation | async-start | bytes 8425472 | tf_op jit(solution)/shard_map/all_gather | solution.py:214
  7.9 23.9 %copy-start.2 = (f32[7,7,704]{2,1,0:T(8,128)S(1)}, f32[7,7,704]{2,1,0:T(8,128)}, u32[]{:S(2)}) copy-start(f32[7,7,704]{2,1,0:T(8,128)} %param.14) | copy-start | bytes 413956
  8.9 23.3 %copy-start = (bf16[24,16,704]{2,1,0:T(8,128)(2,1)S(1)}, bf16[24,16,704]{2,1,0:T(8,128)(2,1)}, u32[]{:S(2)}) copy-start(bf16[24,16,704]{2,1,0:T(8,128)(2,1)} %param.13) | copy-start | bytes 1622020
  8.9 23.2 %collective-permute-start = (bf16[3,16,704]{2,1,0:T(8,128)(2,1)S(1)}, bf16[3,16,704]{2,1,0:T(8,128)(2,1)S(1)}, u32[]{:S(2)}, u32[]{:S(2)}) collective-permute-start(bf16[3,16,704]{2,1,0:T(8,128)(2,1)S(1)} %get-tuple-element.88), channel_id=1, source_target_pairs={{0,8},{8,16},{16,24},{1,9},{9,17},{17,25},{2,10},{10,18},{18,26},{... | collective-permute-start | bytes 202760 | tf_op jit(solution)/shard_map/ppermute | solution.py:23
  12.5 19.7 %collective-permute-start.1 = (bf16[3,16,704]{2,1,0:T(8,128)(2,1)S(1)}, bf16[3,16,704]{2,1,0:T(8,128)(2,1)S(1)}, u32[]{:S(2)}, u32[]{:S(2)}) collective-permute-start(bf16[3,16,704]{2,1,0:T(8,128)(2,1)S(1)} %get-tuple-element.87), channel_id=1, source_target_pairs={{8,0},{16,8},{24,16},{9,1},{17,9},{25,17},{10,2},{18,10},{26,18},{... | collective-permute-start | bytes 202760 | tf_op jit(solution)/shard_map/ppermute | solution.py:26
  31.7 50.3 %copy-start.30 = (f32[256]{0:T(256)}, f32[256]{0:T(256)S(1)}, u32[]{:S(2)}) copy-start(f32[256]{0:T(256)S(1)} %convert_element_type.365) | copy-start | bytes 3076
  32.4 6.9 %collective-permute-start.2 = (bf16[30,3,704]{2,1,0:T(4,128)(2,1)S(1)}, bf16[30,3,704]{2,1,0:T(4,128)(2,1)S(1)}, u32[]{:S(2)}, u32[]{:S(2)}) collective-permute-start(bf16[30,3,704]{2,1,0:T(4,128)(2,1)S(1)} %get-tuple-element.83), channel_id=1, source_target_pairs={{0,2},{2,4},{4,6},{1,3},{3,5},{5,7},{8,10},{10,12},{12,14},{9,11},... | collective-permute-start | bytes 380168 | tf_op jit(solution)/shard_map/ppermute | solution.py:23
  34.3 6.7 %collective-permute-start.3 = (bf16[30,3,704]{2,1,0:T(4,128)(2,1)S(1)}, bf16[30,3,704]{2,1,0:T(4,128)(2,1)S(1)}, u32[]{:S(2)}, u32[]{:S(2)}) collective-permute-start(bf16[30,3,704]{2,1,0:T(4,128)(2,1)S(1)} %get-tuple-element.84), channel_id=1, source_target_pairs={{2,0},{4,2},{6,4},{3,1},{5,3},{7,5},{10,8},{12,10},{14,12},{11,9},... | collective-permute-start | bytes 380168 | tf_op jit(solution)/shard_map/ppermute | solution.py:26
  43.0 17.1 %copy-start.29 = (f32[2816]{0:T(1024)S(1)}, f32[2816]{0:T(1024)}, u32[]{:S(2)}) copy-start(f32[2816]{0:T(1024)} %param.20) | copy-start | bytes 33796
  48.8 17.0 %copy-start.37 = (f32[2816]{0:T(1024)S(1)}, f32[2816]{0:T(1024)}, u32[]{:S(2)}) copy-start(f32[2816]{0:T(1024)} %param.19) | copy-start | bytes 33796
  48.8 17.0 %copy-start.38 = (f32[1408]{0:T(1024)S(1)}, f32[1408]{0:T(1024)}, u32[]{:S(2)}) copy-start(f32[1408]{0:T(1024)} %param.17) | copy-start | bytes 16900
  48.8 17.0 %copy-start.39 = (f32[1408]{0:T(1024)S(1)}, f32[1408]{0:T(1024)}, u32[]{:S(2)}) copy-start(f32[1408]{0:T(1024)} %param.16) | copy-start | bytes 16900
  48.8 15.7 %collective-permute-start.4 = (bf16[256,704]{1,0:T(8,128)(2,1)S(1)}, bf16[256,704]{1,0:T(8,128)(2,1)S(1)}, u32[]{:S(2)}, u32[]{:S(2)}) collective-permute-start(bf16[256,704]{1,0:T(8,128)(2,1)S(1)} %bitcast.65), channel_id=1, source_target_pairs={{0,1},{1,0},{2,3},{3,2},{4,5},{5,4},{6,7},{7,6},{8,9},{9,8},{10,11... | collective-permute-start | bytes 1081352 | tf_op jit(solution)/shard_map/ppermute | solution.py:63
  50.5 23.3 %collective-permute-start.5 = (bf16[256,704]{1,0:T(8,128)(2,1)S(1)}, bf16[256,704]{1,0:T(8,128)(2,1)S(1)}, u32[]{:S(2)}, u32[]{:S(2)}) collective-permute-start(bf16[256,704]{1,0:T(8,128)(2,1)S(1)} %fusion.26), channel_id=1, source_target_pairs={{0,1},{1,0},{2,3},{3,2},{4,5},{5,4},{6,7},{7,6},{8,9},{9,8},{10,11... | collective-permute-start | bytes 1081352 | tf_op jit(solution)/shard_map/ppermute | solution.py:63
  112.8 15.7 %collective-permute-start.6 = (bf16[256,704]{1,0:T(8,128)(2,1)}, bf16[256,704]{1,0:T(8,128)(2,1)}, u32[]{:S(2)}, u32[]{:S(2)}) collective-permute-start(bf16[256,704]{1,0:T(8,128)(2,1)} %dynamic-slice_convert_fusion.1), channel_id=1, source_target_pairs={{0,1},{1,0},{2,3},{3,2},{4,5},{5,4},{6,7},{7,6},{8,9},{9,8},{10,11... | collective-permute-start | bytes 1081352 | tf_op jit(solution)/shard_map/ppermute | solution.py:63
  114.8 20.4 %copy-start.31 = (f32[256]{0:T(256)S(1)}, f32[256]{0:T(256)}, u32[]{:S(2)}) copy-start(f32[256]{0:T(256)} %copy-done.30) | copy-start | bytes 3076
  114.8 20.4 %copy-start.33 = (f32[704]{0:T(1024)S(1)}, f32[704]{0:T(1024)}, u32[]{:S(2)}) copy-start(f32[704]{0:T(1024)} %param.23) | copy-start | bytes 8452
  114.8 20.4 %copy-start.35 = (f32[256]{0:T(256)S(1)}, f32[256]{0:T(256)}, u32[]{:S(2)}) copy-start(f32[256]{0:T(256)} %copy-done.34) | copy-start | bytes 3076
  124.7 3.7 %collective-permute-start.8 = (f32[2,256]{1,0:T(2,128)S(1)}, f32[2,256]{1,0:T(2,128)S(1)}, u32[]{:S(2)}, u32[]{:S(2)}) collective-permute-start(f32[2,256]{1,0:T(2,128)S(1)} %pad_maximum_fusion.9), channel_id=1, source_target_pairs={{0,1},{1,0},{2,3},{3,2},{4,5},{5,4},{6,7},{7,6},{8,9},{9,8},{10,11... | collective-permute-start | bytes 6152 | tf_op jit(solution)/shard_map/ppermute | solution.py:63
  126.3 8.9 %collective-permute-start.7 = (bf16[256,704]{1,0:T(8,128)(2,1)S(1)}, bf16[256,704]{1,0:T(8,128)(2,1)S(1)}, u32[]{:S(2)}, u32[]{:S(2)}) collective-permute-start(bf16[256,704]{1,0:T(8,128)(2,1)S(1)} %dynamic-slice_convert_fusion), channel_id=1, source_target_pairs={{0,1},{1,0},{2,3},{3,2},{4,5},{5,4},{6,7},{7,6},{8,9},{9,8},{10,11... | collective-permute-start | bytes 1081352 | tf_op jit(solution)/shard_map/ppermute | solution.py:63
  137.3 9.5 %collective-permute-start.10 = (bf16[3,16,704]{2,1,0:T(8,128)(2,1)S(1)}, bf16[3,16,704]{2,1,0:T(8,128)(2,1)S(1)}, u32[]{:S(2)}, u32[]{:S(2)}) collective-permute-start(bf16[3,16,704]{2,1,0:T(8,128)(2,1)S(1)} %fusion.90), channel_id=1, source_target_pairs={{8,0},{16,8},{24,16},{9,1},{17,9},{25,17},{10,2},{18,10},{26,18},{... | collective-permute-start | bytes 202760 | tf_op jit(solution)/shard_map/ppermute | solution.py:26
  140.4 6.2 %collective-permute-start.9 = (bf16[3,16,704]{2,1,0:T(8,128)(2,1)S(1)}, bf16[3,16,704]{2,1,0:T(8,128)(2,1)S(1)}, u32[]{:S(2)}, u32[]{:S(2)}) collective-permute-start(bf16[3,16,704]{2,1,0:T(8,128)(2,1)S(1)} %fusion.91), channel_id=1, source_target_pairs={{0,8},{8,16},{16,24},{1,9},{9,17},{17,25},{2,10},{10,18},{18,26},{... | collective-permute-start | bytes 202760 | tf_op jit(solution)/shard_map/ppermute | solution.py:23
  146.9 8.9 %copy-start.4 = (f32[704]{0:T(1024)S(1)}, f32[704]{0:T(1024)}, u32[]{:S(2)}) copy-start(f32[704]{0:T(1024)} %copy-done.3) | copy-start | bytes 8452
  147.0 8.9 %copy-start.6 = (f32[704]{0:T(1024)S(1)}, f32[704]{0:T(1024)}, u32[]{:S(2)}) copy-start(f32[704]{0:T(1024)} %copy-done.5) | copy-start | bytes 8452
  147.0 8.9 %copy-start.8 = (f32[704]{0:T(1024)S(1)}, f32[704]{0:T(1024)}, u32[]{:S(2)}) copy-start(f32[704]{0:T(1024)} %copy-done.7) | copy-start | bytes 8452
  147.0 8.9 %copy-start.10 = (f32[704]{0:T(1024)S(1)}, f32[704]{0:T(1024)}, u32[]{:S(2)}) copy-start(f32[704]{0:T(1024)} %copy-done.9) | copy-start | bytes 8452
  147.0 8.9 %copy-start.12 = (f32[704]{0:T(1024)S(1)}, f32[704]{0:T(1024)}, u32[]{:S(2)}) copy-start(f32[704]{0:T(1024)} %copy-done.11) | copy-start | bytes 8452
  147.0 8.9 %copy-start.14 = (f32[704]{0:T(1024)S(1)}, f32[704]{0:T(1024)}, u32[]{:S(2)}) copy-start(f32[704]{0:T(1024)} %copy-done.13) | copy-start | bytes 8452
  147.0 8.9 %copy-start.16 = (f32[704]{0:T(1024)S(1)}, f32[704]{0:T(1024)}, u32[]{:S(2)}) copy-start(f32[704]{0:T(1024)} %copy-done.15) | copy-start | bytes 8452
  147.1 5.0 %collective-permute-start.11 = (bf16[30,3,704]{2,1,0:T(4,128)(2,1)S(1)}, bf16[30,3,704]{2,1,0:T(4,128)(2,1)S(1)}, u32[]{:S(2)}, u32[]{:S(2)}) collective-permute-start(bf16[30,3,704]{2,1,0:T(4,128)(2,1)S(1)} %get-tuple-element.81), channel_id=1, source_target_pairs={{2,0},{4,2},{6,4},{3,1},{5,3},{7,5},{10,8},{12,10},{14,12},{11,9},... | collective-permute-start | bytes 380168 | tf_op jit(solution)/shard_map/ppermute | solution.py:26
  149.0 6.9 %collective-permute-start.12 = (bf16[30,3,704]{2,1,0:T(4,128)(2,1)S(1)}, bf16[30,3,704]{2,1,0:T(4,128)(2,1)S(1)}, u32[]{:S(2)}, u32[]{:S(2)}) collective-permute-start(bf16[30,3,704]{2,1,0:T(4,128)(2,1)S(1)} %get-tuple-element.82), channel_id=1, source_target_pairs={{0,2},{2,4},{4,6},{1,3},{3,5},{5,7},{8,10},{10,12},{12,14},{9,11},... | collective-permute-start | bytes 380168 | tf_op jit(solution)/shard_map/ppermute | solution.py:23
  (22 other events, 129.3 us)
Sparse Core Ops, SparseCore 0:
  10.2 71.7 all-gather.1

commit v3 on v2

--- a/solution.py
+++ b/solution.py
@@ -15,19 +15,6 @@
 root_two_pi_inv = 0.3989422804014327
 
 
-def extended(block, sides, width):
-    for axis, dim in sides:
-        count = lax.axis_size(axis)
-        forward = [(i, i + 1) for i in range(count - 1)]
-        backward = [(target, source) for source, target in forward]
-        low = lax.ppermute(
-            lax.slice_in_dim(block, block.shape[dim] - width, None, axis=dim), axis, forward
-        )
-        high = lax.ppermute(lax.slice_in_dim(block, 0, width, axis=dim), axis, backward)
-        block = jnp.concatenate([low, block, high], axis=dim)
-    return block
-
-
 def gelu_value(values):
     return 0.5 * values * (1.0 + jax.scipy.special.erf(values * root_half))
 
@@ -39,37 +26,12 @@
     )
 
 
-def depthwise(padded, kernel, rows_out, cols_out, flipped):
-    summed = jnp.zeros((rows_out, cols_out, kernel.shape[2]), jnp.float32)
-    last_tap = KERNEL - 1
-    for row_tap in range(KERNEL):
-        for col_tap in range(KERNEL):
-            row_start = last_tap - row_tap if flipped else row_tap
-            col_start = last_tap - col_tap if flipped else col_tap
-            window = padded[row_start : row_start + rows_out, col_start : col_start + cols_out]
-            summed = summed + window.astype(jnp.float32) * kernel[row_tap, col_tap]
-    return summed
-
-
 MOST = 4
-
-
-def extend(image):
-    return extended(image, (("sy", 0), ("sx", 1)), KERNEL // 2)
 
 
 def swapped(array):
     count = lax.axis_size("tp")
     return lax.ppermute(array, "tp", [(i, count - 1 - i) for i in range(count)])
-
-
-def conv_tiles(windows, kernel):
-    summed = jnp.zeros((windows.shape[0], TILE, TILE, windows.shape[3]), jnp.float32)
-    for row_tap in range(KERNEL):
-        for col_tap in range(KERNEL):
-            window = windows[:, row_tap : row_tap + TILE, col_tap : col_tap + TILE]
-            summed = summed + window.astype(jnp.float32) * kernel[row_tap, col_tap]
-    return summed
 
 
 MESH = pl.DeviceIdType.MESH
@@ -185,6 +147,156 @@
     return scale, slope
 
 
+REACH = KERNEL // 2
+LEFT = 8
+LANES = 128
+
+
+def halo_kernel(
+    sy_count, sx_count, image, strips, sides, ends, corners, send_sems, recv_sems
+):
+    rows = image.shape[0]
+    deep = strips.shape[1]
+    sy = lax.axis_index("sy")
+    sx = lax.axis_index("sx")
+    plan = []
+    for dy in (-1, 0, 1):
+        for dx in (-1, 0, 1):
+            if dy == 0 and dx == 0:
+                continue
+            to_y, to_x = sy + dy, sx + dx
+            there = (to_y >= 0) & (to_y < sy_count) & (to_x >= 0) & (to_x < sx_count)
+            from_y, from_x = sy - dy, sx - dx
+            comes = (from_y >= 0) & (from_y < sy_count) & (from_x >= 0) & (from_x < sx_count)
+            strip = 0 if dx < 0 else 1
+            if dy == 0:
+                source, target = strips.at[strip], sides.at[1 - strip]
+            elif dx == 0:
+                source = image.at[pl.ds(0 if dy < 0 else rows - REACH, REACH)]
+                target = ends.at[1 if dy < 0 else 0]
+            else:
+                source = strips.at[strip, pl.ds(0 if dy < 0 else deep - 16, 16)]
+                target = corners.at[(2 if dy < 0 else 0) + (1 - strip)]
+            plan.append((there, comes, {"sy": to_y, "sx": to_x}, source, target))
+    barrier = pltpu.get_barrier_semaphore()
+    for there, _, place, _, _ in plan:
+
+        @pl.when(there)
+        def _(place=place):
+            pl.semaphore_signal(barrier, inc=1, device_id=place, device_id_type=MESH)
+
+    pl.semaphore_wait(barrier, sum(there.astype(jnp.int32) for there, _, _, _, _ in plan))
+
+    copies = []
+    for number, (there, _, place, source, target) in enumerate(plan):
+        copy = pltpu.make_async_remote_copy(
+            src_ref=source,
+            dst_ref=target,
+            send_sem=send_sems.at[number],
+            recv_sem=recv_sems.at[number],
+            device_id=place,
+            device_id_type=MESH,
+        )
+        copies.append(copy)
+
+        @pl.when(there)
+        def _(copy=copy):
+            copy.start()
+
+    for (there, comes, _, _, target), copy in zip(plan, copies):
+
+        @pl.when(comes)
+        def _(copy=copy):
+            copy.wait_recv()
+
+        @pl.when(jnp.logical_not(comes))
+        def _(target=target):
+            target[...] = jnp.zeros(target.shape, target.dtype)
+
+        @pl.when(there)
+        def _(copy=copy):
+            copy.wait_send()
+
+
+def halo(image, number):
+    rows, cols, width = image.shape
+    strips = jnp.stack([image[:, :REACH], image[:, cols - REACH :]])
+    strips = jnp.pad(strips.reshape(2, rows * REACH, width), ((0, 0), (7, 1), (0, 0)))
+    sy_count = lax.axis_size("sy")
+    sx_count = lax.axis_size("sx")
+    vmem = pl.BlockSpec(memory_space=pltpu.VMEM)
+    return pl.pallas_call(
+        functools.partial(halo_kernel, sy_count, sx_count),
+        out_shape=[
+            jax.ShapeDtypeStruct(strips.shape, image.dtype),
+            jax.ShapeDtypeStruct((2, REACH, cols, width), image.dtype),
+            jax.ShapeDtypeStruct((4, 16, width), image.dtype),
+        ],
+        in_specs=[vmem, vmem],
+        out_specs=[vmem, vmem, vmem],
+        scratch_shapes=[pltpu.SemaphoreType.DMA((8,)), pltpu.SemaphoreType.DMA((8,))],
+        compiler_params=pltpu.CompilerParams(collective_id=number, has_side_effects=True),
+    )(image, strips)
+
+
+def conv_kernel(flipped, image, sides, ends, corners, kernel, extra, out, padded):
+    rows, cols, width = image.shape
+    wide = jnp.float32
+    padded[REACH : REACH + rows, LEFT : LEFT + cols, :] = image[...].astype(wide)
+    for end in range(2):
+        at = 0 if end == 0 else REACH + rows
+        padded[at : at + REACH, LEFT : LEFT + cols, :] = ends[end].astype(wide)
+    for side in range(2):
+        at = LEFT - REACH if side == 0 else LEFT + cols
+        strip = sides[side].astype(wide)
+        for row in range(rows):
+            first = 7 + REACH * row
+            padded[REACH + row, at : at + REACH, :] = strip[first : first + REACH]
+        for end in range(2):
+            corner = corners[end * 2 + side].astype(wide)
+            base = 6 if end == 0 else 7
+            for row in range(REACH):
+                top = row if end == 0 else REACH + rows + row
+                first = base + REACH * row
+                padded[top, at : at + REACH, :] = corner[first : first + REACH]
+
+    def block(step, carry):
+        top = step * TILE
+        for lane in range(0, width, LANES):
+            lanes = slice(lane, min(lane + LANES, width))
+            for col in range(0, cols, TILE):
+                total = None
+                for q in range(KERNEL):
+                    start = col + q + LEFT - REACH
+                    window = padded[pl.ds(top, TILE + KERNEL - 1), start : start + TILE, lanes]
+                    for p in range(KERNEL):
+                        a, b = (KERNEL - 1 - p, KERNEL - 1 - q) if flipped else (p, q)
+                        term = window[p : p + TILE] * kernel[a, b : b + 1, lanes]
+                        total = term if total is None else total + term
+                if flipped:
+                    total = total + extra[pl.ds(top, TILE), col : col + TILE, lanes].astype(wide)
+                else:
+                    total = total + extra[:, lanes]
+                out[pl.ds(top, TILE), col : col + TILE, lanes] = total.astype(out.dtype)
+        return carry
+
+    lax.fori_loop(0, rows // TILE, block, 0)
+
+
+def convolve(image, kernel, extra, flipped, number):
+    rows, cols, width = image.shape
+    sides, ends, corners = halo(image, number)
+    vmem = pl.BlockSpec(memory_space=pltpu.VMEM)
+    return pl.pallas_call(
+        functools.partial(conv_kernel, flipped),
+        out_shape=jax.ShapeDtypeStruct(image.shape, jnp.bfloat16),
+        in_specs=[vmem] * 6,
+        out_specs=vmem,
+        scratch_shapes=[pltpu.VMEM((rows + KERNEL - 1, cols + 2 * LEFT, width), jnp.float32)],
+        compiler_params=pltpu.CompilerParams(vmem_limit_bytes=32 * 1024 * 1024),
+    )(image, sides, ends, corners, kernel, extra)
+
+
 def shards(
     features,
     depth_kernel,
@@ -259,8 +371,8 @@
     masked_cot = (cot_tiles.astype(jnp.float32) * mask_rows[:, None]).astype(jnp.bfloat16)
     cot_wide = both_halves(masked_cot)
 
-    convolved = conv_tiles(windows_of(extend(features), TILE + KERNEL - 1), depth_kernel)
-    convolved = (convolved + depth_bias).astype(jnp.bfloat16).reshape(pixels, local_channels)
+    convolved = convolve(features, depth_kernel, depth_bias[None], False, 1)
+    convolved = windows_of(convolved, TILE).reshape(pixels, local_channels)
     gathered = both_halves(convolved).astype(jnp.float32)
     centre = jnp.mean(gathered, axis=1, keepdims=True)
     spread = jnp.mean(jnp.square(gathered - centre), axis=1, keepdims=True)
@@ -302,10 +414,7 @@
         scaled - (sums[0] / channels)[:, None] - own_standard * (sums[1] / channels)[:, None]
     )
     grad_image = spread_out(convolved_grad.astype(jnp.bfloat16))
-    feature_grad = (
-        cotangent.astype(jnp.float32)
-        + depthwise(extend(grad_image), depth_kernel, image_rows, image_cols, True)
-    ).astype(jnp.bfloat16)
+    feature_grad = convolve(grad_image, depth_kernel, cotangent, True, 2)
 
     addend = spread_out(mask_rows[:, None] * (branch + down_bias))
     block_out = (features.astype(jnp.float32) + addend).astype(jnp.bfloat16)

time: 179 us -> 175 us (0.978)
  Pallas kernels: 13.4 us -> 64.2 us
  other arithmetic: 35.2 us -> 11.9 us
  starting transfers between devices: 26.7 us -> 5.11 us
  waiting for transfers between devices: 26.4 us -> 9.17 us
  local copies, waits for them, and re-layouts: 7.28 us -> 13.2 us
    pallas_call x0 -> x4, Pallas kernels: none -> 50.7 us  [the longest x2 27.5 us: convolve(): pl.pallas_call(functools.partial(conv_kernel, flipped), out_shape=jax.Sha...]
    ppermute x8 -> x0, starting transfers between devices: 21.7 us -> none  [the longest x4 11 us: extended(): lax.ppermute(lax.slice_in_dim(block, 0, width, axis=dim), axis, backward)]
    convert_element_type x2 -> x0, other arithmetic: 20.8 us -> none  [the longest x1 15.1 us: shards(): feature_grad = (cotangent.astype(jnp.float32) + depthwise(extend(grad_ima...]
    ppermute x8 -> x0, waiting for transfers between devices: 9.46 us -> none  [the longest x4 7.2 us: extended(): lax.ppermute(lax.slice_in_dim(block, block.shape[dim] - width, None, axis...]
    unnamed x84 -> x43, local copies, waits for them, and re-layouts: 1.24 us -> 8.55 us
    all_gather x1, waiting for transfers between devices: 8.18 us -> 0.9 us  [shards(): down_t = lax.all_gather(down_weight.T, ('sy', 'sx'), axis=0, tiled=True)]
    pallas_call x2, other arithmetic: 2.66 us -> 0.77 us  [response_scales(): pl.pallas_call(functools.partial(sums_kernel, sx_count, sy_count), out_sh...]
  transfers between devices with their start and end apart: 14 -> 6, of which waited for: 8 -> 3; matrix products, arithmetic and copies ran while one was open for 22% -> 18% of each run, Pallas kernels for 0% -> 16%
where the time goes in v3:
time: 175 us; the launch traced here: 173 us
  Pallas kernels  64.2 us (37%)
  between operations  36.7 us (21%)
  matrix products  32.7 us (19%)
  local copies, waits for them, and re-layouts  13.2 us (8%)
  other arithmetic  11.9 us (7%)
  waiting for transfers between devices  9.17 us (5%)
  starting transfers between devices  5.11 us (3%)
    pallas_call x2, Pallas kernels, convolve(): pl.pallas_call(functools.partial(conv_kernel, flipped), out_shape=jax.Sha...  27.5 us
    pallas_call x2, Pallas kernels, halo(): pl.pallas_call(functools.partial(halo_kernel, sy_count, sx_count), out_sh...  23.2 us
    pallas_call x1, Pallas kernels, response_scales(): pl.pallas_call(functools.partial(sums_kernel, sx_count, sy_count), out_sh...  13.4 us
    dot_general x1, matrix products, shards(): lax.dot_general(preact_grad, up_weight, contract_last, preferred_element_...  10.5 us
    unnamed x43, local copies, waits for them, and re-layouts  8.55 us
    dot_general x1, matrix products, shards(): back_hidden = jnp.dot(cot_wide, down_t, preferred_element_type=jnp.float32)  8.27 us
    dot_general x1, matrix products, shards(): jnp.dot(normed, up_weight, preferred_element_type=jnp.float32) + up_bias  7.78 us
    ppermute x5, waiting for transfers between devices, swapped(): return lax.ppermute(array, 'tp', [(i, count - 1 - i) for i in range(count)])  7.59 us
  transfers between devices with their start and end apart: 6, of which 3 were waited for; matrix products, arithmetic and copies ran while one was open for 18% of the time, Pallas kernels for 16%

profile of v3, /device:TPU:12, one launch (start us, length us, event | category | flops | bytes accessed | tf_op | source)
XLA Modules:
  0.0 172.8 jit_solution(15307051611121396767)
XLA Ops:
  7.9 0.8 copy.27
  8.9 1.3 reduce_sum.148
  11.0 0.8 select_reduce_fusion.8
  22.6 1.2 fusion.61
  24.0 0.8 fusion.39.strips
  24.7 14.7 %shard_map.140 = (bf16[2,80,704]{2,1,0:T(8,128)(2,1)}, bf16[2,3,16,704]{3,2,1,0:T(8,128)(2,1)}, bf16[4,16,704]{2,1,0:T(8,128)(2,1)}) custom-call(bf16[24,16,704]{2,1,0:T(8,128)(2,1)} %image.3, bf16[2,80,704]{2,1,0:T(8,128)(2,1)} %fusion.39.strips), custom_call_target="tpu_custom_call" | custom-call | tf_op jit(solution)/shard_map/pallas_call | solution.py:228
  39.6 0.9 copy-done.5
  40.5 0.9 copy-done.8
  41.4 0.9 copy-done.10
  42.3 13.4 %shard_map.141 = bf16[24,16,704]{2,1,0:T(8,128)(2,1)S(1)} custom-call(bf16[24,16,704]{2,1,0:T(8,128)(2,1)S(1)} %copy-done, bf16[2,80,704]{2,1,0:T(8,128)(2,1)S(1)} %copy-done.5, bf16[2,3,16,704]{3,2,1,0:T(8,128)(2,1)S(1)} %copy-done.8, bf16[4,16,704]{2,1,0:T(8,128)(2,1)S(1)} %copy-done.10, f32[7,7,704]{2,1,0:T(8,128)S(1)} %copy-done.4, ...), custom_call_target="tpu_custom_call" | custom-call | tf_op jit(solution)/shard_map/pallas_call | solution.py:290
  55.9 1.6 collective-permute-start
  57.5 2.5 %add_convert_fusion.2 = f32[4]{0:T(128)S(1)} fusion(s32[1]{0:T(128)} %bitcast.3, s32[1]{0:T(128)} %bitcast.2, s32[1]{0:T(128)} %bitcast.1, s32[1]{0:T(128)} %bitcast), kind=kLoop, calls=%fused_computation.120 | loop fusion | flops 16 | bytes 32 | tf_op jit(solution)/shard_map/convert_element_type | solution.py:335
  75.7 7.8 %convolution_add_fusion = f32[256,2816]{1,0:T(8,128)} fusion(bf16[1408,2816]{1,0:T(8,128)(2,1)} %param.18, f32[2816]{0:T(1024)S(1)} %copy-done.17, f32[1408]{0:T(1024)S(1)} %copy-done.19, f32[1408]{0:T(1024)S(1)} %copy-done.20, f32[256]{0:T(256)S(1)} %add_rsqrt_fusion, f32[256]{0:T(256)S(1)} %broadcast_multiply_fusion, bf16[256,704]{1,0:T(8,128)(2,1)S(1)} %bitcast.68, ...), kind=kOutput, calls=%fused_computation.6 | convolution fusion | flops 2036170752 | bytes 11558913 | tf_op jit(solution)/shard_map/dot_general | solution.py:382
  83.4 0.9 all-gather.2.cloned.1.call-done
  84.3 8.3 %fusion.6 = (f32[2816]{0:T(1024)S(1)}, f32[2816]{0:T(1024)S(1)}, bf16[256,2816]{1,0:T(8,128)(2,1)}, f32[256,2816]{1,0:T(8,128)}) fusion(f32[256]{0:T(256)S(1)} %convert_element_type.65, f32[256,2816]{1,0:T(8,128)} %convolution_add_fusion, bf16[1408,2816]{1,0:T(8,128)(2,1)} %all-gather.2.cloned.1.call-done, bf16[256,704]{1,0:T(8,128)(2,1)S(1)} %collective-permute-done.1, ...), kind=kOutput, calls=%fused_computation.13 | convolution fusion | flops 2041211392 | bytes 15883265 | tf_op jit(solution)/shard_map/dot_general | solution.py:387
  93.3 13.4 %shard_map.142 = (f32[1,2816]{1,0:T(1,128)}, f32[1,2816]{1,0:T(1,128)}) custom-call(f32[1,5632]{1,0:T(1,128)} %broadcast_in_dim.19.vector_ref, f32[1,2816]{1,0:T(1,128)} %broadcast_in_dim.20.gain_ref), custom_call_target="tpu_custom_call" | custom-call | tf_op jit(solution)/shard_map/pallas_call | solution.py:127
  107.4 6.1 %fusion.14 = f32[256,1408]{1,0:T(8,128)S(1)} fusion(bf16[1408,2816]{1,0:T(8,128)(2,1)} %all-gather.2.cloned.1.call-done, bf16[256,2816]{1,0:T(8,128)(2,1)} %get-tuple-element.30, f32[2816]{0:T(1024)S(1)} %copy-done.18, f32[2816]{0:T(1024)S(1)} %reduce.9), kind=kOutput, calls=%fused_computation.26 | convolution fusion | flops 2032926720 | bytes 10835968 | tf_op jit(solution)/shard_map/dot_general | solution.py:392
  113.6 1.1 copy-done.11
  114.9 0.8 collective-permute-start.2
  115.7 10.5 %fusion.59 = (f32[256]{0:T(256)S(1)}, f32[256]{0:T(256)S(1)}, f32[256,1408]{1,0:T(8,128)S(1)}, f32[256,1408]{1,0:T(8,128)S(1)}) fusion(f32[256]{0:T(256)S(1)} %add_rsqrt_fusion, f32[256]{0:T(256)S(1)} %broadcast_multiply_fusion, bf16[256,704]{1,0:T(8,128)(2,1)S(1)} %bitcast.69, bf16[256,704]{1,0:T(8,128)(2,1)S(1)} %collective-permute-done, pred[]{:T(512)S(6)} %eq.40, ...), kind=kOutput, calls=%fused_computation.128 | convolution fusion | flops 2046623232 | bytes 18776576 | tf_op jit(solution)/shard_map/dot_general | solution.py:401
  126.2 1.4 collective-permute-start.4
  127.8 0.8 collective-permute-start.3
  128.5 1.4 collective-permute-done.4
  130.5 6.2 %collective-permute-done.3 = bf16[256,704]{1,0:T(8,128)(2,1)S(1)} collective-permute-done((bf16[256,704]{1,0:T(8,128)(2,1)S(1)}, bf16[256,704]{1,0:T(8,128)(2,1)S(1)}, u32[]{:S(2)}, u32[]{:S(2)}) %collective-permute-start.3) | collective-permute-done | bytes 360480 | tf_op jit(solution)/shard_map/ppermute | solution.py:34
  137.9 0.8 select_maximum_fusion.strips
  138.7 8.5 %shard_map.143 = (bf16[2,80,704]{2,1,0:T(8,128)(2,1)}, bf16[2,3,16,704]{3,2,1,0:T(8,128)(2,1)}, bf16[4,16,704]{2,1,0:T(8,128)(2,1)}) custom-call(bf16[24,16,704]{2,1,0:T(8,128)(2,1)} %copy-done.1, bf16[2,80,704]{2,1,0:T(8,128)(2,1)} %select_maximum_fusion.strips), custom_call_target="tpu_custom_call" | custom-call | tf_op jit(solution)/shard_map/pallas_call | solution.py:228
  147.2 1.1 copy-done.2
  148.2 0.9 copy-done.6
  149.2 0.9 copy-done.7
  150.1 0.9 copy-done.9
  151.0 14.1 %shard_map.144 = bf16[24,16,704]{2,1,0:T(8,128)(2,1)} custom-call(bf16[24,16,704]{2,1,0:T(8,128)(2,1)S(1)} %copy-done.2, bf16[2,80,704]{2,1,0:T(8,128)(2,1)S(1)} %copy-done.6, bf16[2,3,16,704]{3,2,1,0:T(8,128)(2,1)S(1)} %copy-done.7, bf16[4,16,704]{2,1,0:T(8,128)(2,1)S(1)} %copy-done.9, f32[7,7,704]{2,1,0:T(8,128)S(1)} %copy-done.4, ...), custom_call_target="tpu_custom_call" | custom-call | tf_op jit(solution)/shard_map/pallas_call | solution.py:290
  165.1 0.9 fusion.25
  (78 shorter events, 9.7 us)
Async XLA Ops:
  7.2 77.2 %all-gather.2.cloned.1.call-start = ((), (), s32[]{:S(2)}) async-start(), calls=%async_computation | async-start | bytes 8425472 | tf_op jit(solution)/shard_map/all_gather | solution.py:326
  7.9 31.6 %copy-start.16 = (f32[704]{0:T(1024)S(1)}, f32[704]{0:T(1024)}, u32[]{:S(2)}) copy-start(f32[704]{0:T(1024)} %param.15) | copy-start | bytes 8452
  7.9 31.6 %copy-start = (bf16[24,16,704]{2,1,0:T(8,128)(2,1)S(1)}, bf16[24,16,704]{2,1,0:T(8,128)(2,1)}, u32[]{:S(2)}) copy-start(bf16[24,16,704]{2,1,0:T(8,128)(2,1)} %image.3) | copy-start | bytes 1622020
  7.9 31.6 %copy-start.4 = (f32[7,7,704]{2,1,0:T(8,128)S(1)}, f32[7,7,704]{2,1,0:T(8,128)}, u32[]{:S(2)}) copy-start(f32[7,7,704]{2,1,0:T(8,128)} %kernel.3) | copy-start | bytes 413956
  24.7 31.0 %copy-start.3 = (bf16[24,16,704]{2,1,0:T(8,128)(2,1)S(1)}, bf16[24,16,704]{2,1,0:T(8,128)(2,1)}, u32[]{:S(2)}) copy-start(bf16[24,16,704]{2,1,0:T(8,128)(2,1)} %extra.1) | copy-start | bytes 1622020
  39.6 0.9 copy-start.5
  40.5 0.9 copy-start.8
  41.4 0.9 copy-start.10
  55.8 14.1 %copy-start.13 = (f32[2816]{0:T(1024)S(1)}, f32[2816]{0:T(1024)}, u32[]{:S(2)}) copy-start(f32[2816]{0:T(1024)} %param.20) | copy-start | bytes 33796
  55.9 18.4 %collective-permute-start = (bf16[256,704]{1,0:T(8,128)(2,1)S(1)}, bf16[256,704]{1,0:T(8,128)(2,1)S(1)}, u32[]{:S(2)}, u32[]{:S(2)}) collective-permute-start(bf16[256,704]{1,0:T(8,128)(2,1)S(1)} %bitcast.65), channel_id=1, source_target_pairs={{0,1},{1,0},{2,3},{3,2},{4,5},{5,4},{6,7},{7,6},{8,9},{9,8},{10,11... | collective-permute-start | bytes 1081352 | tf_op jit(solution)/shard_map/ppermute | solution.py:34
  60.1 15.5 %copy-start.17 = (f32[2816]{0:T(1024)S(1)}, f32[2816]{0:T(1024)}, u32[]{:S(2)}) copy-start(f32[2816]{0:T(1024)} %param.19) | copy-start | bytes 33796
  60.1 15.5 %copy-start.19 = (f32[1408]{0:T(1024)S(1)}, f32[1408]{0:T(1024)}, u32[]{:S(2)}) copy-start(f32[1408]{0:T(1024)} %param.17) | copy-start | bytes 16900
  60.1 15.5 %copy-start.20 = (f32[1408]{0:T(1024)S(1)}, f32[1408]{0:T(1024)}, u32[]{:S(2)}) copy-start(f32[1408]{0:T(1024)} %param.16) | copy-start | bytes 16900
  60.3 23.1 %collective-permute-start.1 = (bf16[256,704]{1,0:T(8,128)(2,1)S(1)}, bf16[256,704]{1,0:T(8,128)(2,1)S(1)}, u32[]{:S(2)}, u32[]{:S(2)}) collective-permute-start(bf16[256,704]{1,0:T(8,128)(2,1)S(1)} %fusion.26), channel_id=1, source_target_pairs={{0,1},{1,0},{2,3},{3,2},{4,5},{5,4},{6,7},{7,6},{8,9},{9,8},{10,11... | collective-permute-start | bytes 1081352 | tf_op jit(solution)/shard_map/ppermute | solution.py:34
  83.4 24.0 %copy-start.18 = (f32[2816]{0:T(1024)S(1)}, f32[2816]{0:T(1024)}, u32[]{:S(2)}) copy-start(f32[2816]{0:T(1024)} %param.21) | copy-start | bytes 33796
  107.4 8.2 %copy-start.14 = (f32[1,2816]{1,0:T(1,128)S(1)}, f32[1,2816]{1,0:T(1,128)}, u32[]{:S(2)}) copy-start(f32[1,2816]{1,0:T(1,128)} %get-tuple-element.14) | copy-start | bytes 33796
  113.6 1.1 copy-start.11
  114.9 15.1 %collective-permute-start.2 = (bf16[256,704]{1,0:T(8,128)(2,1)S(1)}, bf16[256,704]{1,0:T(8,128)(2,1)S(1)}, u32[]{:S(2)}, u32[]{:S(2)}) collective-permute-start(bf16[256,704]{1,0:T(8,128)(2,1)S(1)} %dynamic-slice_convert_fusion.1), channel_id=1, source_target_pairs={{0,1},{1,0},{2,3},{3,2},{4,5},{5,4},{6,7},{7,6},{8,9},{9,8},{10,11... | collective-permute-start | bytes 1081352 | tf_op jit(solution)/shard_map/ppermute | solution.py:34
  115.7 14.3 %copy-start.12 = (f32[256,1408]{1,0:T(8,128)S(1)}, f32[256,1408]{1,0:T(8,128)}, u32[]{:S(2)}) copy-start(f32[256,1408]{1,0:T(8,128)} %copy-done.11) | copy-start | bytes 4325380
  115.7 14.3 %copy-start.15 = (f32[704]{0:T(1024)S(1)}, f32[704]{0:T(1024)}, u32[]{:S(2)}) copy-start(f32[704]{0:T(1024)} %param.23) | copy-start | bytes 8452
  126.2 3.7 %collective-permute-start.4 = (f32[2,256]{1,0:T(2,128)S(1)}, f32[2,256]{1,0:T(2,128)S(1)}, u32[]{:S(2)}, u32[]{:S(2)}) collective-permute-start(f32[2,256]{1,0:T(2,128)S(1)} %pad_maximum_fusion.3), channel_id=1, source_target_pairs={{0,1},{1,0},{2,3},{3,2},{4,5},{5,4},{6,7},{7,6},{8,9},{9,8},{10,11... | collective-permute-start | bytes 6152 | tf_op jit(solution)/shard_map/ppermute | solution.py:34
  127.8 8.9 %collective-permute-start.3 = (bf16[256,704]{1,0:T(8,128)(2,1)S(1)}, bf16[256,704]{1,0:T(8,128)(2,1)S(1)}, u32[]{:S(2)}, u32[]{:S(2)}) collective-permute-start(bf16[256,704]{1,0:T(8,128)(2,1)S(1)} %dynamic-slice_convert_fusion), channel_id=1, source_target_pairs={{0,1},{1,0},{2,3},{3,2},{4,5},{5,4},{6,7},{7,6},{8,9},{9,8},{10,11... | collective-permute-start | bytes 1081352 | tf_op jit(solution)/shard_map/ppermute | solution.py:34
  137.5 1.1 copy-start.1
  147.2 1.1 copy-start.2
  148.2 0.9 copy-start.6
  149.2 0.9 copy-start.7
  150.1 0.9 copy-start.9
Sparse Core Ops, SparseCore 0:
  10.2 74.1 all-gather.1

commit v4 on v3

--- a/solution.py
+++ b/solution.py
@@ -297,6 +297,41 @@
     )(image, sides, ends, corners, kernel, extra)
 
 
+def gradient_conv(image, kernel, cotangent, sent):
+    rows, cols, width = image.shape
+    sides, ends, corners = halo(image, 2)
+    sides, sent = lax.optimization_barrier((sides, sent))
+    came = swapped(sent)
+    sides = sides[:, 7 : 7 + REACH * rows].reshape(2, rows, REACH, width)
+    above = corners[:2, 6:15].reshape(2, REACH, REACH, width)
+    below = corners[2:, 7:16].reshape(2, REACH, REACH, width)
+    columns = [
+        jnp.concatenate([above[0], sides[0], below[0]], axis=0),
+        jnp.concatenate([ends[0], image, ends[1]], axis=0),
+        jnp.concatenate([above[1], sides[1], below[1]], axis=0),
+    ]
+    padded = jnp.concatenate(columns, axis=1)
+    side = TILE + KERNEL - 1
+    windows = jnp.stack(
+        [
+            padded[row : row + side, col : col + side]
+            for row in range(0, rows, TILE)
+            for col in range(0, cols, TILE)
+        ]
+    )
+    summed = jnp.zeros((windows.shape[0], TILE, TILE, width), jnp.float32)
+    last_tap = KERNEL - 1
+    for row_tap in range(KERNEL):
+        for col_tap in range(KERNEL):
+            window = windows[:, row_tap : row_tap + TILE, col_tap : col_tap + TILE]
+            summed = summed + window.astype(jnp.float32) * kernel[
+                last_tap - row_tap, last_tap - col_tap
+            ]
+    summed = summed.reshape(rows // TILE, cols // TILE, TILE, TILE, width)
+    summed = summed.transpose(0, 2, 1, 3, 4).reshape(rows, cols, width)
+    return (cotangent.astype(jnp.float32) + summed).astype(jnp.bfloat16), came
+
+
 def shards(
     features,
     depth_kernel,
@@ -388,14 +423,6 @@
     products = jnp.sum(back_hidden * hidden_wide, axis=0)
     scale, slope = response_scales(squares, products, response_gain)
 
-    response = (hidden_wide * scale + response_shift).astype(jnp.bfloat16)
-    partial_out = lax.dot_general(
-        response, down_t, contract_last, preferred_element_type=jnp.float32
-    )
-    sent_out = lax.dynamic_slice_in_dim(partial_out, other_start, local_channels, 1)
-    kept_out = lax.dynamic_slice_in_dim(partial_out, channel_start, local_channels, 1)
-    branch = kept_out + swapped(sent_out.astype(jnp.bfloat16)).astype(jnp.float32)
-
     hidden_grad = back_hidden * scale + slope * mask_rows[:, None] * hidden_wide
     preact_grad = (hidden_grad * gelu_slope(preact)).astype(jnp.bfloat16)
     grad_terms = lax.dot_general(
@@ -409,12 +436,24 @@
     sent_grad = lax.dynamic_slice_in_dim(scaled_terms, other_start, local_channels, 1)
     kept_grad = lax.dynamic_slice_in_dim(scaled_terms, channel_start, local_channels, 1)
     own_standard = lax.dynamic_slice_in_dim(standard, channel_start, local_channels, 1)
-    scaled = kept_grad + swapped(sent_grad.astype(jnp.bfloat16)).astype(jnp.float32)
+    sent_grad, held_hidden = lax.optimization_barrier((sent_grad.astype(jnp.bfloat16), hidden))
+    came_grad = swapped(sent_grad)
+    response = (held_hidden.astype(jnp.float32) * scale + response_shift).astype(jnp.bfloat16)
+    partial_out = lax.dot_general(
+        response, down_t, contract_last, preferred_element_type=jnp.float32
+    )
+    sent_out = lax.dynamic_slice_in_dim(partial_out, other_start, local_channels, 1)
+    kept_out = lax.dynamic_slice_in_dim(partial_out, channel_start, local_channels, 1)
+
+    scaled = kept_grad + came_grad.astype(jnp.float32)
     convolved_grad = inv_scale * (
         scaled - (sums[0] / channels)[:, None] - own_standard * (sums[1] / channels)[:, None]
     )
     grad_image = spread_out(convolved_grad.astype(jnp.bfloat16))
-    feature_grad = convolve(grad_image, depth_kernel, cotangent, True, 2)
+    feature_grad, came_out = gradient_conv(
+        grad_image, depth_kernel, cotangent, sent_out.astype(jnp.bfloat16)
+    )
+    branch = kept_out + came_out.astype(jnp.float32)
 
     addend = spread_out(mask_rows[:, None] * (branch + down_bias))
     block_out = (features.astype(jnp.float32) + addend).astype(jnp.bfloat16)

time: 175 us -> 166 us (0.949)
  Pallas kernels: 64.2 us -> 50.8 us
  other arithmetic: 11.9 us -> 22.7 us
  matrix products: 32.7 us -> 29.2 us
  local copies, waits for them, and re-layouts: 13.2 us -> 10.6 us
    pallas_call x2 -> x1, Pallas kernels: 27.5 us -> 14.1 us  [convolve(): pl.pallas_call(functools.partial(conv_kernel, flipped), out_shape=jax.Sha...]
    add x0 -> x1, other arithmetic: none -> 8.13 us  [gradient_conv(): summed + window.astype(jnp.float32) * kernel[last_tap - row_tap, last_tap...]
    dot_general x1, matrix products: 6.13 us -> 2.43 us  [shards(): lax.dot_general(response, down_t, contract_last, preferred_element_type=j...]
    unnamed x43 -> x44, local copies, waits for them, and re-layouts: 8.55 us -> 5.11 us
  transfers between devices with their start and end apart: 6 -> 6, of which waited for: 3 -> 2; matrix products, arithmetic and copies ran while one was open for 18% -> 20% of each run, Pallas kernels for 16% -> 17%
where the time goes in v4:
time: 166 us; the launch traced here: 165 us
  Pallas kernels  50.8 us (31%)
  between operations  36.8 us (22%)
  matrix products  29.2 us (18%)
  other arithmetic  22.7 us (14%)
  local copies, waits for them, and re-layouts  10.6 us (6%)
  waiting for transfers between devices  8.89 us (5%)
  starting transfers between devices  5.84 us (4%)
    pallas_call x2, Pallas kernels, halo(): pl.pallas_call(functools.partial(halo_kernel, sy_count, sx_count), out_sh...  24.7 us
    pallas_call x1, Pallas kernels, convolve(): pl.pallas_call(functools.partial(conv_kernel, flipped), out_shape=jax.Sha...  14.1 us
    pallas_call x1, Pallas kernels, response_scales(): pl.pallas_call(functools.partial(sums_kernel, sx_count, sy_count), out_sh...  12 us
    dot_general x1, matrix products, shards(): lax.dot_general(preact_grad, up_weight, contract_last, preferred_element_...  10.7 us
    dot_general x1, matrix products, shards(): back_hidden = jnp.dot(cot_wide, down_t, preferred_element_type=jnp.float32)  8.29 us
    ppermute x5, waiting for transfers between devices, swapped(): return lax.ppermute(array, 'tp', [(i, count - 1 - i) for i in range(count)])  8.21 us
    add x1, other arithmetic, gradient_conv(): summed + window.astype(jnp.float32) * kernel[last_tap - row_tap, last_tap...  8.13 us
    dot_general x1, matrix products, shards(): jnp.dot(normed, up_weight, preferred_element_type=jnp.float32) + up_bias  7.78 us
  transfers between devices with their start and end apart: 6, of which 2 were waited for; matrix products, arithmetic and copies ran while one was open for 20% of the time, Pallas kernels for 17%

profile of v4, /device:TPU:12, one launch (start us, length us, event | category | flops | bytes accessed | tf_op | source)
XLA Modules:
  0.0 164.8 jit_solution(17984604923432794270)
XLA Ops:
  7.2 0.7 all-gather.2.cloned.1.call-update
  7.9 0.8 copy.29
  9.0 1.3 reduce_sum.148
  10.9 0.8 select_reduce_fusion.8
  22.5 1.2 fusion.66
  24.0 0.8 fusion.44.strips
  24.7 14.7 %shard_map.140 = (bf16[2,80,704]{2,1,0:T(8,128)(2,1)}, bf16[2,3,16,704]{3,2,1,0:T(8,128)(2,1)}, bf16[4,16,704]{2,1,0:T(8,128)(2,1)}) custom-call(bf16[24,16,704]{2,1,0:T(8,128)(2,1)} %image.3, bf16[2,80,704]{2,1,0:T(8,128)(2,1)} %fusion.44.strips), custom_call_target="tpu_custom_call" | custom-call | tf_op jit(solution)/shard_map/pallas_call | solution.py:228
  39.5 2.5 %add_convert_fusion.5 = f32[4]{0:T(128)S(1)} fusion(s32[1]{0:T(128)} %bitcast.3, s32[1]{0:T(128)} %bitcast.2, s32[1]{0:T(128)} %bitcast.1, s32[1]{0:T(128)} %bitcast), kind=kLoop, calls=%fused_computation.192 | loop fusion | flops 16 | bytes 32 | tf_op jit(solution)/shard_map/convert_element_type | solution.py:370
  42.1 0.9 copy-done.2
  43.1 0.9 copy-done.3
  44.0 0.9 copy-done.4
  44.9 14.1 %shard_map.141 = bf16[24,16,704]{2,1,0:T(8,128)(2,1)S(1)} custom-call(bf16[24,16,704]{2,1,0:T(8,128)(2,1)S(1)} %copy-done, bf16[2,80,704]{2,1,0:T(8,128)(2,1)S(1)} %copy-done.2, bf16[2,3,16,704]{3,2,1,0:T(8,128)(2,1)S(1)} %copy-done.3, bf16[4,16,704]{2,1,0:T(8,128)(2,1)S(1)} %copy-done.4, f32[7,7,704]{2,1,0:T(8,128)S(1)} %copy-done.1, ...), custom_call_target="tpu_custom_call" | custom-call | tf_op jit(solution)/shard_map/pallas_call | solution.py:290
  59.3 1.6 collective-permute-start
  75.4 3.4 %collective-permute-done.1 = bf16[256,704]{1,0:T(8,128)(2,1)S(1)} collective-permute-done((bf16[256,704]{1,0:T(8,128)(2,1)S(1)}, bf16[256,704]{1,0:T(8,128)(2,1)S(1)}, u32[]{:S(2)}, u32[]{:S(2)}) %collective-permute-start.1) | collective-permute-done | bytes 360480 | tf_op jit(solution)/shard_map/ppermute | solution.py:34
  79.4 0.7 fusion.11
  80.1 7.8 %convolution_add_fusion = f32[256,2816]{1,0:T(8,128)} fusion(bf16[1408,2816]{1,0:T(8,128)(2,1)} %param.18, f32[2816]{0:T(1024)S(1)} %copy-done.16, f32[1408]{0:T(1024)S(1)} %copy-done.18, f32[1408]{0:T(1024)S(1)} %copy-done.19, f32[256]{0:T(256)S(1)} %add_rsqrt_fusion, f32[256]{0:T(256)S(1)} %broadcast_multiply_fusion, bf16[256,704]{1,0:T(8,128)(2,1)S(1)} %bitcast.102, ...), kind=kOutput, calls=%fused_computation.5 | convolution fusion | flops 2036170752 | bytes 11558913 | tf_op jit(solution)/shard_map/dot_general | solution.py:417
  87.9 8.3 %fusion.6 = (f32[2816]{0:T(1024)S(1)}, f32[2816]{0:T(1024)S(1)}, bf16[256,2816]{1,0:T(8,128)(2,1)}, f32[256,2816]{1,0:T(8,128)}) fusion(f32[256]{0:T(256)S(1)} %convert_element_type.221, f32[256,2816]{1,0:T(8,128)} %convolution_add_fusion, bf16[1408,2816]{1,0:T(8,128)(2,1)} %all-gather.2.cloned.1.call-done, bf16[256,704]{1,0:T(8,128)(2,1)S(1)} %collective-permute-done, ...), kind=kOutput, calls=%fused_computation.12 | convolution fusion | flops 2041211392 | bytes 15883265 | tf_op jit(solution)/shard_map/dot_general | solution.py:422
  96.8 12.0 %shard_map.142 = (f32[1,2816]{1,0:T(1,128)}, f32[1,2816]{1,0:T(1,128)}) custom-call(f32[1,5632]{1,0:T(1,128)} %broadcast_in_dim.19.vector_ref, f32[1,2816]{1,0:T(1,128)} %broadcast_in_dim.20.gain_ref), custom_call_target="tpu_custom_call" | custom-call | tf_op jit(solution)/shard_map/pallas_call | solution.py:127
  108.8 0.7 reduce.10
  109.5 0.7 reduce.9
  110.3 10.7 %fusion.64 = (f32[256]{0:T(256)S(1)}, f32[256]{0:T(256)S(1)}, f32[256,1408]{1,0:T(8,128)S(1)}, f32[256,1408]{1,0:T(8,128)S(1)}) fusion(f32[256]{0:T(256)S(1)} %add_rsqrt_fusion, f32[256]{0:T(256)S(1)} %broadcast_multiply_fusion, bf16[256,704]{1,0:T(8,128)(2,1)S(1)} %bitcast.103, bf16[256,704]{1,0:T(8,128)(2,1)S(1)} %collective-permute-done.1, ...), kind=kOutput, calls=%fused_computation.200 | convolution fusion | flops 2046623232 | bytes 18776576 | tf_op jit(solution)/shard_map/dot_general | solution.py:428
  121.8 1.6 collective-permute-start.2
  123.4 2.4 %fusion.12 = f32[256,1408]{1,0:T(8,128)S(1)} fusion(bf16[1408,2816]{1,0:T(8,128)(2,1)S(1)} %copy-done.15, bf16[256,2816]{1,0:T(8,128)(2,1)S(1)} %copy-done.20, f32[2816]{0:T(1024)S(1)} %copy-done.17, f32[2816]{0:T(1024)S(1)} %reduce.9), kind=kOutput, calls=%fused_computation.24 | convolution fusion | flops 2032926720 | bytes 10835968 | tf_op jit(solution)/shard_map/dot_general | solution.py:442
  126.0 4.8 %collective-permute-done.2 = bf16[256,704]{1,0:T(8,128)(2,1)S(1)} collective-permute-done((bf16[256,704]{1,0:T(8,128)(2,1)S(1)}, bf16[256,704]{1,0:T(8,128)(2,1)S(1)}, u32[]{:S(2)}, u32[]{:S(2)}) %collective-permute-start.2) | collective-permute-done | bytes 360480 | tf_op jit(solution)/shard_map/ppermute | solution.py:34
  130.9 0.7 multiply_convert_fusion.1
  132.1 0.8 select_maximum_fusion.strips
  132.9 10.0 %shard_map.143 = (bf16[2,80,704]{2,1,0:T(8,128)(2,1)}, bf16[2,3,16,704]{3,2,1,0:T(8,128)(2,1)}, bf16[4,16,704]{2,1,0:T(8,128)(2,1)}) custom-call(bf16[24,16,704]{2,1,0:T(8,128)(2,1)} %copy-done.5, bf16[2,80,704]{2,1,0:T(8,128)(2,1)} %select_maximum_fusion.strips), custom_call_target="tpu_custom_call" | custom-call | tf_op jit(solution)/shard_map/pallas_call | solution.py:228
  142.9 0.9 bitcast_dynamic-update-slice_fusion.1
  145.2 1.5 collective-permute-start.4
  146.7 8.1 %multiply_add_fusion = f32[6,8,8,704]{3,2,1,0:T(8,128)S(1)} fusion(bf16[6,14,14,704]{3,2,1,0:T(8,128)(2,1)S(1)} %fusion.35, f32[704]{0:T(1024)S(1)} %get-tuple-element.77, f32[704]{0:T(1024)S(1)} %get-tuple-element.78, f32[704]{0:T(1024)S(1)} %get-tuple-element.31, f32[704]{0:T(1024)S(1)} %get-tuple-element.32, f32[704]{0:T(1024)S(1)} %get-tuple-element.33, ...), kind=kLoop, calls=%fused_computation.44 | loop fusion | flops 39469056 | bytes 27712256 | tf_op jit(solution)/shard_map/add | solution.py:327
  155.0 1.0 add_convert_fusion.3
  157.0 0.9 fusion.22
  (102 shorter events, 9.8 us)
Async XLA Ops:
  7.2 80.8 %all-gather.2.cloned.1.call-start = ((), (), s32[]{:S(2)}) async-start(), calls=%async_computation | async-start | bytes 8425472 | tf_op jit(solution)/shard_map/all_gather | solution.py:361
  22.5 17.0 %copy-start.14 = (f32[704]{0:T(1024)S(1)}, f32[704]{0:T(1024)}, u32[]{:S(2)}) copy-start(f32[704]{0:T(1024)} %param.15) | copy-start | bytes 8452
  22.5 19.6 %copy-start = (bf16[24,16,704]{2,1,0:T(8,128)(2,1)S(1)}, bf16[24,16,704]{2,1,0:T(8,128)(2,1)}, u32[]{:S(2)}) copy-start(bf16[24,16,704]{2,1,0:T(8,128)(2,1)} %image.3) | copy-start | bytes 1622020
  22.5 19.6 %copy-start.1 = (f32[7,7,704]{2,1,0:T(8,128)S(1)}, f32[7,7,704]{2,1,0:T(8,128)}, u32[]{:S(2)}) copy-start(f32[7,7,704]{2,1,0:T(8,128)} %kernel.1) | copy-start | bytes 413956
  24.7 34.3 %copy-start.6 = (bf16[24,16,704]{2,1,0:T(8,128)(2,1)S(1)}, bf16[24,16,704]{2,1,0:T(8,128)(2,1)}, u32[]{:S(2)}) copy-start(bf16[24,16,704]{2,1,0:T(8,128)(2,1)} %param.25) | copy-start | bytes 1622020
  42.1 0.9 copy-start.2
  43.1 0.9 copy-start.3
  44.0 0.9 copy-start.4
  59.1 11.4 %copy-start.12 = (f32[2816]{0:T(1024)S(1)}, f32[2816]{0:T(1024)}, u32[]{:S(2)}) copy-start(f32[2816]{0:T(1024)} %param.20) | copy-start | bytes 33796
  59.3 28.6 %collective-permute-start = (bf16[256,704]{1,0:T(8,128)(2,1)S(1)}, bf16[256,704]{1,0:T(8,128)(2,1)S(1)}, u32[]{:S(2)}, u32[]{:S(2)}) collective-permute-start(bf16[256,704]{1,0:T(8,128)(2,1)S(1)} %fusion.23), channel_id=1, source_target_pairs={{0,1},{1,0},{2,3},{3,2},{4,5},{5,4},{6,7},{7,6},{8,9},{9,8},{10,11... | collective-permute-start | bytes 1081352 | tf_op jit(solution)/shard_map/ppermute | solution.py:34
  60.9 19.2 %copy-start.16 = (f32[2816]{0:T(1024)S(1)}, f32[2816]{0:T(1024)}, u32[]{:S(2)}) copy-start(f32[2816]{0:T(1024)} %param.19) | copy-start | bytes 33796
  60.9 19.2 %copy-start.18 = (f32[1408]{0:T(1024)S(1)}, f32[1408]{0:T(1024)}, u32[]{:S(2)}) copy-start(f32[1408]{0:T(1024)} %param.17) | copy-start | bytes 16900
  61.0 19.2 %copy-start.19 = (f32[1408]{0:T(1024)S(1)}, f32[1408]{0:T(1024)}, u32[]{:S(2)}) copy-start(f32[1408]{0:T(1024)} %param.16) | copy-start | bytes 16900
  61.0 17.8 %collective-permute-start.1 = (bf16[256,704]{1,0:T(8,128)(2,1)S(1)}, bf16[256,704]{1,0:T(8,128)(2,1)S(1)}, u32[]{:S(2)}, u32[]{:S(2)}) collective-permute-start(bf16[256,704]{1,0:T(8,128)(2,1)S(1)} %bitcast.99), channel_id=1, source_target_pairs={{0,1},{1,0},{2,3},{3,2},{4,5},{5,4},{6,7},{7,6},{8,9},{9,8},{10,11... | collective-permute-start | bytes 1081352 | tf_op jit(solution)/shard_map/ppermute | solution.py:34
  110.3 13.1 %copy-start.15 = (bf16[1408,2816]{1,0:T(8,128)(2,1)S(1)}, bf16[1408,2816]{1,0:T(8,128)(2,1)}, u32[]{:S(2)}) copy-start(bf16[1408,2816]{1,0:T(8,128)(2,1)} %all-gather.2.cloned.1.call-done) | copy-start | bytes 23789572
  110.3 13.1 %copy-start.17 = (f32[2816]{0:T(1024)S(1)}, f32[2816]{0:T(1024)}, u32[]{:S(2)}) copy-start(f32[2816]{0:T(1024)} %param.21) | copy-start | bytes 33796
  110.3 13.0 %copy-start.20 = (bf16[256,2816]{1,0:T(8,128)(2,1)S(1)}, bf16[256,2816]{1,0:T(8,128)(2,1)}, u32[]{:S(2)}) copy-start(bf16[256,2816]{1,0:T(8,128)(2,1)} %get-tuple-element.19) | copy-start | bytes 4325380
  121.0 5.0 %collective-permute-start.3 = (f32[2,256]{1,0:T(2,128)S(1)}, f32[2,256]{1,0:T(2,128)S(1)}, u32[]{:S(2)}, u32[]{:S(2)}) collective-permute-start(f32[2,256]{1,0:T(2,128)S(1)} %pad_maximum_fusion.9), channel_id=1, source_target_pairs={{0,1},{1,0},{2,3},{3,2},{4,5},{5,4},{6,7},{7,6},{8,9},{9,8},{10,11... | collective-permute-start | bytes 6152 | tf_op jit(solution)/shard_map/ppermute | solution.py:34
  121.8 9.1 %collective-permute-start.2 = (bf16[256,704]{1,0:T(8,128)(2,1)S(1)}, bf16[256,704]{1,0:T(8,128)(2,1)S(1)}, u32[]{:S(2)}, u32[]{:S(2)}) collective-permute-start(bf16[256,704]{1,0:T(8,128)(2,1)S(1)} %dynamic-slice_convert_fusion.1), channel_id=1, source_target_pairs={{0,1},{1,0},{2,3},{3,2},{4,5},{5,4},{6,7},{7,6},{8,9},{9,8},{10,11... | collective-permute-start | bytes 1081352 | tf_op jit(solution)/shard_map/ppermute | solution.py:34
  125.8 5.7 %copy-start.7 = (f32[256,1408]{1,0:T(8,128)}, f32[256,1408]{1,0:T(8,128)S(1)}, u32[]{:S(2)}) copy-start(f32[256,1408]{1,0:T(8,128)S(1)} %fusion.12) | copy-start | bytes 4325380
  131.8 1.1 copy-start.5
  142.9 1.1 copy-start.10
  142.9 1.1 copy-start.9
  142.9 1.2 copy-start.11
  145.2 10.8 %collective-permute-start.4 = (bf16[256,704]{1,0:T(8,128)(2,1)S(1)}, bf16[256,704]{1,0:T(8,128)(2,1)S(1)}, u32[]{:S(2)}, u32[]{:S(2)}) collective-permute-start(bf16[256,704]{1,0:T(8,128)(2,1)S(1)} %dynamic-slice_convert_fusion), channel_id=1, source_target_pairs={{0,1},{1,0},{2,3},{3,2},{4,5},{5,4},{6,7},{7,6},{8,9},{9,8},{10,11... | collective-permute-start | bytes 1081352 | tf_op jit(solution)/shard_map/ppermute | solution.py:34
  155.0 1.6 copy-start.8
  155.0 1.6 copy-start.13
Sparse Core Ops, SparseCore 0:
  10.2 74.1 all-gather.1
